TPU v7x, 32 devices: a whole 2x2x4 slice. The times are simulated.
32 devices in a mesh: shard: 2 (over core), ctx: 4 (over y, x), tp: 4 (over z).
Axes of the slice: x: 2, y: 2, z: 4, core: 2. Of those that a mesh axis runs over, the one named last changes fastest.
Arguments:
- inputs: bfloat16 [2, 1024, 1024], P('shard', 'ctx', 'tp'), may hold values from -6 to 6
- w_query: bfloat16 [1024, 2048], P('shard', 'tp'), may hold values from -0.1875 to 0.1875
- key_weight: bfloat16 [1024, 1024], P('shard', 'tp'), may hold values from -0.1875 to 0.1875
- value_weight: bfloat16 [1024, 1024], P('shard', 'tp'), may hold values from -0.1875 to 0.1875
- w_out: bfloat16 [2048, 1024], P('tp', 'shard'), may hold values from -3 to 3
- w_gate: bfloat16 [1024, 3072], P('shard', 'tp'), may hold values from -0.1875 to 0.1875
- w_up: bfloat16 [1024, 3072], P('shard', 'tp'), may hold values from -0.1875 to 0.1875
- w_down: bfloat16 [3072, 1024], P('tp', 'shard'), may hold values from -0.109375 to 0.109375
- norm_attn: bfloat16 [1024], P('shard'), may hold values from 0.5 to 1.5
- norm_mlp: bfloat16 [1024], P('shard'), may hold values from 0.5 to 1.5
- gain_query: bfloat16 [128], P('shard'), may hold values from 0.099609375 to 1.8984375
- gain_key: bfloat16 [128], P('shard'), may hold values from 0.099609375 to 1.8984375
- cotangent: bfloat16 [2, 1024, 1024], P('shard', 'ctx', 'tp'), may hold values from -6 to 6
Outputs:
- outputs: bfloat16 [2, 1024, 1024], P('shard', 'ctx', 'tp')
- d_inputs: bfloat16 [2, 1024, 1024], P('shard', 'ctx', 'tp')
- d_query: float32 [1024, 2048], P(('shard', 'ctx'), 'tp')
- d_key: float32 [1024, 1024], P(('shard', 'ctx'), 'tp')
- d_value: float32 [1024, 1024], P(('shard', 'ctx'), 'tp')
- d_out: float32 [2048, 1024], P('tp', ('shard', 'ctx'))
- d_gate: float32 [1024, 3072], P(('shard', 'ctx'), 'tp')
- d_up: float32 [1024, 3072], P(('shard', 'ctx'), 'tp')
- d_down: float32 [3072, 1024], P('tp', ('shard', 'ctx'))
- d_norm_attn: float32 [1024], P(('shard', 'ctx'))
- d_norm_mlp: float32 [1024], P(('shard', 'ctx'))
- d_gain_query: float32 [128], P(('shard', 'ctx'))
- d_gain_key: float32 [128], P(('shard', 'ctx'))
All inputs are finite; a program needn't handle non-finite values.
Results may differ from a plain program's by a relative error of at most 0.025.
Values may be sent and summed in bfloat16 or wider, within the bound.
A program may use at most 128 MiB of HBM per device.

v0:
```python
from functools import partial

import jax
import jax.numpy as jnp
from jax import lax
from jax.sharding import PartitionSpec as P

HEAD_SIZE = 128


epsilon = 1e-06
rope_base = 1000000.0
masked_score = -1e30


def rms_norm(value_rows, gain_row):
    return (
        value_rows
        * lax.rsqrt(jnp.mean(value_rows * value_rows, axis=-1, keepdims=True) + epsilon)
        * gain_row
    )


def rms_back(value_rows, gain_row, grad_in):
    factor = lax.rsqrt(jnp.mean(value_rows * value_rows, axis=-1, keepdims=True) + epsilon)
    unit_rows = value_rows * factor
    weighted = grad_in * gain_row
    d_values = factor * (
        weighted - unit_rows * jnp.mean(weighted * unit_rows, axis=-1, keepdims=True)
    )
    return (d_values, jnp.sum(grad_in * unit_rows, axis=0))


def rotary(value_rows, positions):
    half_dim = value_rows.shape[-1] // 2
    frequency = jnp.power(
        rope_base, -(jnp.arange(half_dim).astype(jnp.float32) * 2.0 / value_rows.shape[-1])
    )
    angles = positions[:, None] * frequency[None, :]
    cosine = jnp.concatenate([jnp.cos(angles), jnp.cos(angles)], axis=-1)[:, None, :]
    sine_part = jnp.concatenate([jnp.sin(angles), jnp.sin(angles)], axis=-1)[:, None, :]
    turned = jnp.concatenate([-value_rows[..., half_dim:], value_rows[..., :half_dim]], axis=-1)
    return value_rows * cosine + turned * sine_part


def head_prep(projected, gain_row, positions):
    tokens = projected.shape[0]
    shaped = projected.reshape(tokens, -1, HEAD_SIZE)
    return rotary(rms_norm(shaped, gain_row), positions).reshape(tokens, -1)


def query_block(array, head_index, heads_per_group):
    tokens = array.shape[0]
    piece = array[
        :, head_index * heads_per_group * HEAD_SIZE : (head_index + 1) * heads_per_group * HEAD_SIZE
    ]
    return (
        piece.reshape(tokens, heads_per_group, HEAD_SIZE)
        .transpose(1, 0, 2)
        .reshape(heads_per_group * tokens, HEAD_SIZE)
    )


def block_back(rows_in, heads_per_group):
    tokens = rows_in.shape[0] // heads_per_group
    return (
        rows_in.reshape(heads_per_group, tokens, HEAD_SIZE)
        .transpose(1, 0, 2)
        .reshape(tokens, heads_per_group * HEAD_SIZE)
    )


def body(
    inputs,
    w_query,
    key_weight,
    value_weight,
    w_out,
    w_gate,
    w_up,
    w_down,
    norm_attn,
    norm_mlp,
    gain_query,
    gain_key,
    cotangent,
):
    (
        w_query,
        key_weight,
        value_weight,
        w_out,
        w_gate,
        w_up,
        w_down,
        norm_attn,
        norm_mlp,
        gain_query,
        gain_key,
    ) = (
        lax.all_gather(w_query, "shard", axis=0, tiled=True),
        lax.all_gather(key_weight, "shard", axis=0, tiled=True),
        lax.all_gather(value_weight, "shard", axis=0, tiled=True),
        lax.all_gather(w_out, "shard", axis=1, tiled=True),
        lax.all_gather(w_gate, "shard", axis=0, tiled=True),
        lax.all_gather(w_up, "shard", axis=0, tiled=True),
        lax.all_gather(w_down, "shard", axis=1, tiled=True),
        lax.all_gather(norm_attn, "shard", axis=0, tiled=True),
        lax.all_gather(norm_mlp, "shard", axis=0, tiled=True),
        lax.all_gather(gain_query, "shard", axis=0, tiled=True),
        lax.all_gather(gain_key, "shard", axis=0, tiled=True),
    )
    norm_attn = norm_attn.astype(jnp.float32)
    norm_mlp = norm_mlp.astype(jnp.float32)
    gain_query = gain_query.astype(jnp.float32)
    gain_key = gain_key.astype(jnp.float32)
    local_tokens = inputs.shape[1]
    width_part = inputs.shape[2]
    feature_start = lax.axis_index("tp") * width_part
    offset = lax.axis_index("ctx") * local_tokens
    query_pos = offset + jnp.arange(local_tokens, dtype=jnp.int32)
    positions = query_pos.astype(jnp.float32)
    full_in = lax.all_gather(inputs, "tp", axis=2, tiled=True).reshape(local_tokens, -1)
    resid_in = full_in.astype(jnp.float32)
    normed_low = rms_norm(resid_in, norm_attn).astype(jnp.bfloat16)
    query_proj = jnp.dot(normed_low, w_query, preferred_element_type=jnp.float32)
    key_proj = jnp.dot(normed_low, key_weight, preferred_element_type=jnp.float32)
    value_proj = jnp.dot(normed_low, value_weight, preferred_element_type=jnp.float32)
    query_pull_fn = partial(head_prep, positions=positions)
    query_heads, query_pull = jax.vjp(query_pull_fn, query_proj, gain_query)
    key_heads, key_pull = jax.vjp(query_pull_fn, key_proj, gain_key)
    query_low = query_heads.astype(jnp.bfloat16)
    key_low = key_heads.astype(jnp.bfloat16)
    value_low = value_proj.astype(jnp.bfloat16)
    key_all, value_all = (
        lax.all_gather(key_low, "ctx", axis=0, tiled=True),
        lax.all_gather(value_low, "ctx", axis=0, tiled=True),
    )
    kv_local = key_low.shape[1] // HEAD_SIZE
    heads_per_group = query_low.shape[1] // (HEAD_SIZE * kv_local)
    seq_len = key_all.shape[0]
    key_pos = jnp.arange(seq_len, dtype=jnp.int32)
    causal = jnp.tile(query_pos[:, None] >= key_pos[None, :], (heads_per_group, 1))
    score_scale = HEAD_SIZE ** (-0.5)

    def head_scores(head_index):
        head_rows = query_block(query_low, head_index, heads_per_group)
        head_keys = key_all[:, head_index * HEAD_SIZE : (head_index + 1) * HEAD_SIZE]
        scores = (
            jnp.einsum("qd,kd->qk", head_rows, head_keys, preferred_element_type=jnp.float32)
            * score_scale
        )
        return (head_rows, head_keys, jnp.where(causal, scores, masked_score))

    attended_parts = []
    row_maxima = []
    row_totals = []
    for head_index in range(kv_local):
        head_rows, head_keys, scores = head_scores(head_index)
        row_max = jnp.max(scores, axis=1, keepdims=True)
        exp_scores = jnp.exp(scores - row_max)
        row_total = jnp.sum(exp_scores, axis=1, keepdims=True)
        probs_low = (exp_scores / row_total).astype(jnp.bfloat16)
        head_values = value_all[:, head_index * HEAD_SIZE : (head_index + 1) * HEAD_SIZE]
        head_out = jnp.dot(probs_low, head_values, preferred_element_type=jnp.float32)
        attended_parts.append(block_back(head_out, heads_per_group))
        row_maxima.append(row_max)
        row_totals.append(row_total)
    attended_low = jnp.concatenate(attended_parts, axis=1).astype(jnp.bfloat16)
    attn_part = jnp.dot(attended_low, w_out, preferred_element_type=jnp.float32)
    mixed = resid_in + lax.psum(attn_part.astype(jnp.bfloat16), "tp").astype(jnp.float32)
    normed_mlp_low = rms_norm(mixed, norm_mlp).astype(jnp.bfloat16)
    gate_act = jnp.dot(normed_mlp_low, w_gate, preferred_element_type=jnp.float32)
    up_act = jnp.dot(normed_mlp_low, w_up, preferred_element_type=jnp.float32)
    hidden_low = (jax.nn.silu(gate_act) * up_act).astype(jnp.bfloat16)
    mlp_part = jnp.dot(hidden_low, w_down, preferred_element_type=jnp.float32)
    result = mixed + lax.psum(mlp_part.astype(jnp.bfloat16), "tp").astype(jnp.float32)
    outputs = (
        lax.dynamic_slice_in_dim(result, feature_start, width_part, 1)
        .astype(jnp.bfloat16)
        .reshape(1, local_tokens, width_part)
    )
    grad_out = lax.all_gather(cotangent, "tp", axis=2, tiled=True).reshape(local_tokens, -1)
    d_down = jnp.einsum("tf,td->fd", hidden_low, grad_out, preferred_element_type=jnp.float32)
    d_hidden = jnp.einsum("td,fd->tf", grad_out, w_down, preferred_element_type=jnp.float32)
    sigmoid_gate = jax.nn.sigmoid(gate_act)
    d_gate_low = (
        d_hidden * up_act * sigmoid_gate * (1.0 + gate_act * (1.0 - sigmoid_gate))
    ).astype(jnp.bfloat16)
    d_up_low = (d_hidden * gate_act * sigmoid_gate).astype(jnp.bfloat16)
    d_gate = jnp.einsum("td,tf->df", normed_mlp_low, d_gate_low, preferred_element_type=jnp.float32)
    d_up = jnp.einsum("td,tf->df", normed_mlp_low, d_up_low, preferred_element_type=jnp.float32)
    d_normed_mlp = jnp.einsum("tf,df->td", d_gate_low, w_gate, preferred_element_type=jnp.float32)
    d_normed_mlp = d_normed_mlp + jnp.einsum(
        "tf,df->td", d_up_low, w_up, preferred_element_type=jnp.float32
    )
    d_normed_mlp = lax.psum(d_normed_mlp.astype(jnp.bfloat16), "tp").astype(jnp.float32)
    d_mix_norm, d_norm_mlp = rms_back(mixed, norm_mlp, d_normed_mlp)
    d_mixed = grad_out.astype(jnp.float32) + d_mix_norm
    d_mixed_low = d_mixed.astype(jnp.bfloat16)
    d_out = jnp.einsum("th,td->hd", attended_low, d_mixed_low, preferred_element_type=jnp.float32)
    d_attended = jnp.einsum(
        "td,hd->th", d_mixed_low, w_out, preferred_element_type=jnp.float32
    ).astype(jnp.bfloat16)
    d_query_parts = []
    d_key_parts = []
    d_value_parts = []
    for head_index in range(kv_local):
        head_rows, head_keys, scores = head_scores(head_index)
        probs_full = jnp.exp(scores - row_maxima[head_index]) / row_totals[head_index]
        probs_low = probs_full.astype(jnp.bfloat16)
        head_values = value_all[:, head_index * HEAD_SIZE : (head_index + 1) * HEAD_SIZE]
        d_rows = query_block(d_attended, head_index, heads_per_group)
        d_probs = jnp.einsum("qd,kd->qk", d_rows, head_values, preferred_element_type=jnp.float32)
        d_value_parts.append(
            jnp.einsum("qk,qd->kd", probs_low, d_rows, preferred_element_type=jnp.float32)
        )
        inner_sum = jnp.sum(probs_full * d_probs, axis=1, keepdims=True)
        d_scores = (probs_full * (d_probs - inner_sum)).astype(jnp.bfloat16)
        d_head_rows = jnp.dot(d_scores, head_keys, preferred_element_type=jnp.float32) * score_scale
        d_query_parts.append(block_back(d_head_rows, heads_per_group))
        d_key_parts.append(
            jnp.einsum("qk,qd->kd", d_scores, head_rows, preferred_element_type=jnp.float32)
            * score_scale
        )
    d_query_heads = jnp.concatenate(d_query_parts, axis=1)
    d_keys_all = jnp.concatenate(d_key_parts, axis=1)
    d_values_all = jnp.concatenate(d_value_parts, axis=1)
    d_key_heads, d_value_proj = (
        lax.psum_scatter(
            d_keys_all.astype(jnp.bfloat16), "ctx", scatter_dimension=0, tiled=True
        ).astype(jnp.float32),
        lax.psum_scatter(
            d_values_all.astype(jnp.bfloat16), "ctx", scatter_dimension=0, tiled=True
        ).astype(jnp.float32),
    )
    d_query_proj, d_gain_query = query_pull(d_query_heads)
    d_key_proj, d_gain_key = key_pull(d_key_heads)
    d_query_low = d_query_proj.astype(jnp.bfloat16)
    d_key_low = d_key_proj.astype(jnp.bfloat16)
    d_value_low = d_value_proj.astype(jnp.bfloat16)
    d_query = jnp.einsum("td,th->dh", normed_low, d_query_low, preferred_element_type=jnp.float32)
    d_key = jnp.einsum("td,th->dh", normed_low, d_key_low, preferred_element_type=jnp.float32)
    d_value = jnp.einsum("td,th->dh", normed_low, d_value_low, preferred_element_type=jnp.float32)
    d_normed = jnp.einsum("th,dh->td", d_query_low, w_query, preferred_element_type=jnp.float32)
    d_normed = d_normed + jnp.einsum(
        "th,dh->td", d_key_low, key_weight, preferred_element_type=jnp.float32
    )
    d_normed = d_normed + jnp.einsum(
        "th,dh->td", d_value_low, value_weight, preferred_element_type=jnp.float32
    )
    d_normed, d_gain_query, d_gain_key = (
        lax.psum(d_normed.astype(jnp.bfloat16), "tp").astype(jnp.float32),
        lax.psum(d_gain_query.astype(jnp.bfloat16), "tp").astype(jnp.float32),
        lax.psum(d_gain_key.astype(jnp.bfloat16), "tp").astype(jnp.float32),
    )
    d_in_norm, d_norm_attn = rms_back(resid_in, norm_attn, d_normed)
    d_full = d_mixed + d_in_norm
    d_inputs = (
        lax.dynamic_slice_in_dim(d_full, feature_start, width_part, 1)
        .astype(jnp.bfloat16)
        .reshape(1, local_tokens, width_part)
    )
    gradients = (
        d_query,
        d_key,
        d_value,
        d_out,
        d_gate,
        d_up,
        d_down,
        d_norm_attn,
        d_norm_mlp,
        d_gain_query,
        d_gain_key,
    )
    gradients = (
        lax.psum_scatter(
            d_query.astype(jnp.bfloat16), ("shard", "ctx"), scatter_dimension=0, tiled=True
        ).astype(jnp.float32),
        lax.psum_scatter(
            d_key.astype(jnp.bfloat16), ("shard", "ctx"), scatter_dimension=0, tiled=True
        ).astype(jnp.float32),
        lax.psum_scatter(
            d_value.astype(jnp.bfloat16), ("shard", "ctx"), scatter_dimension=0, tiled=True
        ).astype(jnp.float32),
        lax.psum_scatter(
            d_out.astype(jnp.bfloat16), ("shard", "ctx"), scatter_dimension=1, tiled=True
        ).astype(jnp.float32),
        lax.psum_scatter(
            d_gate.astype(jnp.bfloat16), ("shard", "ctx"), scatter_dimension=0, tiled=True
        ).astype(jnp.float32),
        lax.psum_scatter(
            d_up.astype(jnp.bfloat16), ("shard", "ctx"), scatter_dimension=0, tiled=True
        ).astype(jnp.float32),
        lax.psum_scatter(
            d_down.astype(jnp.bfloat16), ("shard", "ctx"), scatter_dimension=1, tiled=True
        ).astype(jnp.float32),
        lax.psum_scatter(
            d_norm_attn.astype(jnp.bfloat16), ("shard", "ctx"), scatter_dimension=0, tiled=True
        ).astype(jnp.float32),
        lax.psum_scatter(
            d_norm_mlp.astype(jnp.bfloat16), ("shard", "ctx"), scatter_dimension=0, tiled=True
        ).astype(jnp.float32),
        lax.psum_scatter(
            d_gain_query.astype(jnp.bfloat16), ("shard", "ctx"), scatter_dimension=0, tiled=True
        ).astype(jnp.float32),
        lax.psum_scatter(
            d_gain_key.astype(jnp.bfloat16), ("shard", "ctx"), scatter_dimension=0, tiled=True
        ).astype(jnp.float32),
    )
    return (outputs, d_inputs) + tuple(gradients)


def solution(mesh):
    return jax.shard_map(
        body,
        mesh=mesh,
        in_specs=(
            P("shard", "ctx", "tp"),
            P("shard", "tp"),
            P("shard", "tp"),
            P("shard", "tp"),
            P("tp", "shard"),
            P("shard", "tp"),
            P("shard", "tp"),
            P("tp", "shard"),
            P("shard"),
            P("shard"),
            P("shard"),
            P("shard"),
            P("shard", "ctx", "tp"),
        ),
        out_specs=(
            P("shard", "ctx", "tp"),
            P("shard", "ctx", "tp"),
            P(("shard", "ctx"), "tp"),
            P(("shard", "ctx"), "tp"),
            P(("shard", "ctx"), "tp"),
            P("tp", ("shard", "ctx")),
            P(("shard", "ctx"), "tp"),
            P(("shard", "ctx"), "tp"),
            P("tp", ("shard", "ctx")),
            P(("shard", "ctx")),
            P(("shard", "ctx")),
            P(("shard", "ctx")),
            P(("shard", "ctx")),
        ),
        check_vma=False,
    )
```

profile of v0, /device:TPU:0, one launch (start us, length us, event | category | flops | bytes accessed | tf_op | source)
XLA Modules:
  0.0 636.8 jit_solution(18001718152559082996)
XLA Ops:
  8.8 17.6 %all_gather.45 = bf16[1,256,1024]{2,1,0:T(8,128)(2,1)S(1)} all-gather(bf16[1,256,256]{2,1,0:T(8,128)(2,1)} %param.13), channel_id=1, replica_groups=mesh['shard'=2,'ctx'=4,'tp'=4] {'tp'}, dimensions={2}, use_global_device_ids=true | all-gather | bytes 655360 | tf_op jit(solution)/shard_map/all_gather | solution.py:123
  36.1 14.3 %all_gather.51 = bf16[1024,256]{0,1:T(8,128)(2,1)S(1)} all-gather(bf16[256,256]{0,1:T(8,128)(2,1)S(1)} %bitcast.179), channel_id=1, replica_groups=mesh['shard'=2,'ctx'=4,'tp'=4] {'ctx'}, dimensions={0}, use_global_device_ids=true | all-gather | bytes 655360 | tf_op jit(solution)/shard_map/all_gather | solution.py:136
  53.9 10.0 %all_gather.53 = bf16[1024,256]{1,0:T(8,128)(2,1)S(1)} all-gather(bf16[256,256]{1,0:T(8,128)(2,1)S(1)} %convolution_convert_fusion.12), channel_id=1, replica_groups=mesh['shard'=2,'ctx'=4,'tp'=4] {'ctx'}, dimensions={0}, use_global_device_ids=true | all-gather | bytes 655360 | tf_op jit(solution)/shard_map/all_gather | solution.py:137
  86.7 22.8 %all_gather.59 = bf16[1,256,1024]{2,1,0:T(8,128)(2,1)} all-gather(bf16[1,256,256]{2,1,0:T(8,128)(2,1)S(1)} %copy-done.46), channel_id=1, replica_groups=mesh['shard'=2,'ctx'=4,'tp'=4] {'tp'}, dimensions={2}, use_global_device_ids=true | all-gather | bytes 655360 | tf_op jit(solution)/shard_map/all_gather | solution.py:183
  109.5 19.0 %all-reduce.18.cloned.1.call-done = bf16[256,1024]{1,0:T(8,128)(2,1)} async-done(((bf16[256,1024]{1,0:T(8,128)(2,1)}), bf16[256,1024]{1,0:T(8,128)(2,1)}) %all-reduce.18.cloned.1.call-update) | async-done | bytes 524304 | tf_op jit(solution)/shard_map/psum | solution.py:171
  131.6 8.1 %all-gather.12.cloned.1.call-done = bf16[1024,768]{1,0:T(8,128)(2,1)} async-done(((bf16[512,768]{1,0:T(8,128)(2,1)}), bf16[1024,768]{1,0:T(8,128)(2,1)}) %all-gather.12.cloned.1.call-update) | async-done | bytes 1572880 | tf_op jit(solution)/shard_map/all_gather | solution.py:105
  142.6 9.5 %all-gather.14.cloned.1.call-done = bf16[1024,768]{1,0:T(8,128)(2,1)} async-done(((bf16[512,768]{1,0:T(8,128)(2,1)}), bf16[1024,768]{1,0:T(8,128)(2,1)}) %all-gather.14.cloned.1.call-update) | async-done | bytes 1572880 | tf_op jit(solution)/shard_map/all_gather | solution.py:106
  155.0 9.5 %all-gather.16.cloned.1.call-done = bf16[768,1024]{1,0:T(8,128)(2,1)} async-done(((bf16[768,512]{1,0:T(8,128)(2,1)}), bf16[768,1024]{1,0:T(8,128)(2,1)}) %all-gather.16.cloned.1.call-update) | async-done | bytes 1572880 | tf_op jit(solution)/shard_map/all_gather | solution.py:107
  164.5 3.7 multiply_convert_fusion.4
  171.4 39.6 %all-reduce.20.cloned.1.call-done = bf16[256,1024]{1,0:T(8,128)(2,1)} async-done(((bf16[256,1024]{1,0:T(8,128)(2,1)}), bf16[256,1024]{1,0:T(8,128)(2,1)}) %all-reduce.20.cloned.1.call-update) | async-done | bytes 524304 | tf_op jit(solution)/shard_map/psum | solution.py:197
  213.3 2.9 fusion.15
  245.6 5.9 reduce-scatter.14.cloned.1.call-done
  253.1 26.2 %reduce-scatter.16.cloned.1.call-done = bf16[256,256]{0,1:T(8,128)(2,1)} async-done(((bf16[1024,256]{0,1:T(8,128)(2,1)}), bf16[256,256]{0,1:T(8,128)(2,1)}) %reduce-scatter.16.cloned.1.call-update) | async-done | bytes 131088 | tf_op jit(solution)/shard_map/reduce_scatter | solution.py:233
  293.5 2.9 convolution_convert_fusion.8
  302.4 15.9 %reduce-scatter.28.cloned.1.call-done = bf16[128,512]{1,0:T(8,128)(2,1)} async-done(((bf16[1024,512]{1,0:T(8,128)(2,1)}), bf16[128,512]{1,0:T(8,128)(2,1)}) %reduce-scatter.28.cloned.1.call-update) | async-done | bytes 131088
  320.1 37.5 %reduce-scatter.18.cloned.1.call-done = bf16[128,512]{1,0:T(8,128)(2,1)} async-done(((bf16[1024,512]{1,0:T(8,128)(2,1)}), bf16[128,512]{1,0:T(8,128)(2,1)}) %reduce-scatter.18.cloned.1.call-update) | async-done | bytes 131088 | tf_op jit(solution)/shard_map/reduce_scatter | solution.py:278
  359.2 35.4 %reduce-scatter.22.cloned.1.call-done = bf16[128,256]{1,0:T(8,128)(2,1)} async-done(((bf16[1024,256]{1,0:T(8,128)(2,1)}), bf16[128,256]{1,0:T(8,128)(2,1)}) %reduce-scatter.22.cloned.1.call-update) | async-done | bytes 65552 | tf_op jit(solution)/shard_map/reduce_scatter | solution.py:284
  396.1 36.1 %reduce-scatter.20.cloned.1.call-done = bf16[128,256]{1,0:T(8,128)(2,1)} async-done(((bf16[1024,256]{1,0:T(8,128)(2,1)}), bf16[128,256]{1,0:T(8,128)(2,1)}) %reduce-scatter.20.cloned.1.call-update) | async-done | bytes 65552 | tf_op jit(solution)/shard_map/reduce_scatter | solution.py:281
  433.7 40.1 %reduce-scatter.30.cloned.1.call-done = bf16[128,768]{1,0:T(8,128)(2,1)} async-done(((bf16[1024,768]{1,0:T(8,128)(2,1)}), bf16[128,768]{1,0:T(8,128)(2,1)}) %reduce-scatter.30.cloned.1.call-update) | async-done | bytes 196624
  475.7 39.7 %reduce-scatter.24.cloned.1.call-done = bf16[128,768]{1,0:T(8,128)(2,1)} async-done(((bf16[1024,768]{1,0:T(8,128)(2,1)}), bf16[128,768]{1,0:T(8,128)(2,1)}) %reduce-scatter.24.cloned.1.call-update) | async-done | bytes 196624 | tf_op jit(solution)/shard_map/reduce_scatter | solution.py:290
  517.2 52.8 %all-reduce.22.cloned.1.call-done = (bf16[256,1024]{1,0:T(8,128)(2,1)}, bf16[256,1024]{1,0:T(8,128)(2,1)}) async-done(((bf16[256,1024]{1,0:T(8,128)(2,1)}, bf16[256,1024]{1,0:T(8,128)(2,1)}), (bf16[256,1024]{1,0:T(8,128)(2,1)}, bf16[256,1024]{1,0:T(8,128)(2,1)})) %all-reduce.22.cloned.1.call-update) | async-done | bytes 1048592 | tf_op jit(solution)/shard_map/psum | solution.py:177
  572.4 14.7 %all-reduce.10 = (bf16[1024]{0:T(1024)(128)(2,1)S(1)}, bf16[1024]{0:T(1024)(128)(2,1)S(1)}, bf16[128]{0:T(256)(128)(2,1)S(1)}, bf16[128]{0:T(256)(128)(2,1)S(1)}) all-reduce(bf16[1024]{0:T(1024)(128)(2,1)S(1)} %get-tuple-element.15, ...), channel_id=11, replica_groups=mesh['shard'=2,'ctx'=4,'tp'=4] {'shard','ctx'}, use_global_device_ids=true, to_apply=%region_28.29.clone | all-reduce | flops 2304 | bytes 9216
  587.2 24.1 %reduce-scatter.26.cloned.1.call-done = bf16[128,768]{1,0:T(8,128)(2,1)} async-done(((bf16[1024,768]{1,0:T(8,128)(2,1)}), bf16[128,768]{1,0:T(8,128)(2,1)}) %reduce-scatter.26.cloned.1.call-update) | async-done | bytes 196624 | tf_op jit(solution)/shard_map/reduce_scatter | solution.py:293
  613.0 11.7 %all-reduce.11 = (bf16[16]{0:T(256)(128)(2,1)S(1)}, bf16[16]{0:T(256)(128)(2,1)S(1)}) all-reduce(bf16[16]{0:T(256)(128)(2,1)S(1)} %dynamic-slice.7, bf16[16]{0:T(256)(128)(2,1)S(1)} %dynamic-slice.9), channel_id=1, replica_groups=mesh['shard'=2,'ctx'=4,'tp'=4] {'tp'}, use_global_device_ids=true, to_apply=%region_32.33 | all-reduce | flops 32 | bytes 128 | tf_op jit(solution)/shard_map/psum | solution.py:254
  (306 shorter events, 120.0 us)
Async XLA Ops:
  7.2 56.8 %all-gather.8.cloned.1.call-start = ((), (), s32[]{:S(2)}) async-start(), calls=%async_computation.9 | async-start | bytes 1572864 | tf_op jit(solution)/shard_map/all_gather | solution.py:101
  7.9 72.5 %all-gather.10.cloned.1.call-start = ((), (), s32[]{:S(2)}) async-start(), calls=%async_computation.10 | async-start | bytes 1572864 | tf_op jit(solution)/shard_map/all_gather | solution.py:104
  8.7 119.8 %all-reduce.18.cloned.1.call-start = ((), (), s32[]{:S(2)}) async-start(), calls=%async_computation.11 | async-start | bytes 1048576 | tf_op jit(solution)/shard_map/psum | solution.py:171
  26.6 39.1 %copy-start.56 = (f32[256]{0:T(256)}, f32[256]{0:T(256)S(1)}, u32[]{:S(2)}) copy-start(f32[256]{0:T(256)S(1)} %add_rsqrt_fusion.1) | copy-start | bytes 3076
  35.9 30.5 %copy-start.22 = (f32[256,128]{0,1:T(8,128)}, f32[256,128]{0,1:T(8,128)S(1)}, u32[]{:S(2)}) copy-start(f32[256,128]{0,1:T(8,128)S(1)} %get-tuple-element.66) | copy-start | bytes 393220
  83.1 56.6 %all-gather.12.cloned.1.call-start = ((), (), s32[]{:S(2)}) async-start(), calls=%async_computation.12 | async-start | bytes 2359296 | tf_op jit(solution)/shard_map/all_gather | solution.py:105
  83.7 68.4 %all-gather.14.cloned.1.call-start = ((), (), s32[]{:S(2)}) async-start(), calls=%async_computation.13 | async-start | bytes 2359296 | tf_op jit(solution)/shard_map/all_gather | solution.py:106
  84.2 80.2 %all-gather.16.cloned.1.call-start = ((), (), s32[]{:S(2)}) async-start(), calls=%async_computation.14 | async-start | bytes 2359296 | tf_op jit(solution)/shard_map/all_gather | solution.py:107
  84.8 126.1 %all-reduce.20.cloned.1.call-start = ((), (), s32[]{:S(2)}) async-start(), calls=%async_computation.15 | async-start | bytes 1048576 | tf_op jit(solution)/shard_map/psum | solution.py:197
  171.4 80.1 %reduce-scatter.14.cloned.1.call-start = ((), (), s32[]{:S(2)}) async-start(), calls=%async_computation.16 | async-start | bytes 655360 | tf_op jit(solution)/shard_map/reduce_scatter | solution.py:230
  226.5 52.8 %reduce-scatter.16.cloned.1.call-start = ((), (), s32[]{:S(2)}) async-start(), calls=%async_computation.17 | async-start | bytes 655360 | tf_op jit(solution)/shard_map/reduce_scatter | solution.py:233
  229.4 88.9 %reduce-scatter.28.cloned.1.call-start = ((), (), s32[]{:S(2)}) async-start(), calls=%async_computation.23 | async-start | bytes 1179648
  236.4 121.2 %reduce-scatter.18.cloned.1.call-start = ((), (), s32[]{:S(2)}) async-start(), calls=%async_computation.18 | async-start | bytes 1179648 | tf_op jit(solution)/shard_map/reduce_scatter | solution.py:278
  245.5 36.0 %copy-start.62 = (f32[128]{0:T(128)S(1)}, f32[128]{0:T(128)}, u32[]{:S(2)}) copy-start(f32[128]{0:T(128)} %copy-done.61) | copy-start | bytes 1540
  245.5 149.1 %reduce-scatter.22.cloned.1.call-start = ((), (), s32[]{:S(2)}) async-start(), calls=%async_computation.20 | async-start | bytes 589824 | tf_op jit(solution)/shard_map/reduce_scatter | solution.py:284
  251.4 30.1 %copy-start.28 = (bf16[256,256]{0,1:T(8,128)(2,1)S(1)}, bf16[256,256]{0,1:T(8,128)(2,1)}, u32[]{:S(2)}) copy-start(bf16[256,256]{0,1:T(8,128)(2,1)} %reduce-scatter.14.cloned.1.call-done) | copy-start | bytes 393220
  281.5 150.7 %reduce-scatter.20.cloned.1.call-start = ((), (), s32[]{:S(2)}) async-start(), calls=%async_computation.19 | async-start | bytes 589824 | tf_op jit(solution)/shard_map/reduce_scatter | solution.py:281
  286.8 187.0 %reduce-scatter.30.cloned.1.call-start = ((), (), s32[]{:S(2)}) async-start(), calls=%async_computation.24 | async-start | bytes 1769472
  291.5 223.9 %reduce-scatter.24.cloned.1.call-start = ((), (), s32[]{:S(2)}) async-start(), calls=%async_computation.21 | async-start | bytes 1769472 | tf_op jit(solution)/shard_map/reduce_scatter | solution.py:290
  293.4 276.5 %all-reduce.22.cloned.1.call-start = ((), (), s32[]{:S(2)}) async-start(), calls=%async_computation.25 | async-start | bytes 2097152 | tf_op jit(solution)/shard_map/psum | solution.py:177
  298.7 312.7 %reduce-scatter.26.cloned.1.call-start = ((), (), s32[]{:S(2)}) async-start(), calls=%async_computation.22 | async-start | bytes 1769472 | tf_op jit(solution)/shard_map/reduce_scatter | solution.py:293
  474.9 97.5 %copy-start.63 = (bf16[1024]{0:T(1024)(128)(2,1)S(1)}, bf16[1024]{0:T(1024)(128)(2,1)}, u32[]{:S(2)}) copy-start(bf16[1024]{0:T(1024)(128)(2,1)} %get-tuple-element.13) | copy-start | bytes 6148
  474.9 97.5 %copy-start.67 = (bf16[128]{0:T(256)(128)(2,1)S(1)}, bf16[128]{0:T(256)(128)(2,1)}, u32[]{:S(2)}) copy-start(bf16[128]{0:T(256)(128)(2,1)} %get-tuple-element.19) | copy-start | bytes 772
  475.0 97.4 %copy-start.68 = (bf16[128]{0:T(256)(128)(2,1)S(1)}, bf16[128]{0:T(256)(128)(2,1)}, u32[]{:S(2)}) copy-start(bf16[128]{0:T(256)(128)(2,1)} %get-tuple-element.17) | copy-start | bytes 772
  (68 other events, 286.5 us)
Sparse Core Ops, SparseCore 0:
  9.6 11.7 all-gather.7
  22.9 10.2 all-gather.9
  83.2 45.2 all-reduce.17
  129.9 9.7 all-gather.11
  141.1 10.9 all-gather.13
  153.5 10.9 all-gather.15
  171.5 39.4 all-reduce.19
  226.6 24.7 reduce-scatter.13
  254.5 24.7 reduce-scatter.15
  282.3 35.9 reduce-scatter.27
  321.5 36.0 reduce-scatter.17
  360.5 34.0 reduce-scatter.21
  398.0 34.1 reduce-scatter.19
  435.4 38.4 reduce-scatter.29
  477.0 38.4 reduce-scatter.23
  517.7 52.1 all-reduce.21
  573.4 37.8 reduce-scatter.25
where the time goes:
time: 638 us; the launch traced here: 637 us
  waiting for transfers between devices  403 us (63%)
  blocking collectives  101 us (16%)
  matrix products  47.5 us (7%)
  other arithmetic  39.4 us (6%)
  local copies, waits for them, and re-layouts  28.2 us (4%)
  between operations  16.9 us (3%)
    unnamed x19, waiting for transfers between devices  59.2 us
    psum x1, waiting for transfers between devices, body(): lax.psum(mlp_part.astype(jnp.bfloat16), 'tp').astype(jnp.float32)  52.8 us
    reduce_scatter x1, waiting for transfers between devices, body(): lax.psum_scatter(d_gate.astype(jnp.bfloat16), ('shard', 'ctx'), scatter_d...  39.7 us
    psum x1, waiting for transfers between devices, body(): lax.psum(d_normed_mlp.astype(jnp.bfloat16), 'tp').astype(jnp.float32)  39.6 us
    reduce_scatter x1, waiting for transfers between devices, body(): lax.psum_scatter(d_query.astype(jnp.bfloat16), ('shard', 'ctx'), scatter_...  37.5 us
    reduce_scatter x1, waiting for transfers between devices, body(): lax.psum_scatter(d_key.astype(jnp.bfloat16), ('shard', 'ctx'), scatter_di...  36.1 us
    reduce_scatter x1, waiting for transfers between devices, body(): lax.psum_scatter(d_value.astype(jnp.bfloat16), ('shard', 'ctx'), scatter_...  35.4 us
    reduce_scatter x1, waiting for transfers between devices, body(): lax.psum_scatter(d_values_all.astype(jnp.bfloat16), 'ctx', scatter_dimens...  26.2 us
  transfers between devices with their start and end apart: 17, of which 15 were waited for; matrix products, arithmetic and copies ran while one was open for 12% of the time, Pallas kernels for 0%

commit v1 on v0

--- a/solution.py
+++ b/solution.py
@@ -3,6 +3,8 @@
 import jax
 import jax.numpy as jnp
 from jax import lax
+from jax.experimental import pallas as pl
+from jax.experimental.pallas import tpu as pltpu
 from jax.sharding import PartitionSpec as P
 
 HEAD_SIZE = 128
@@ -70,7 +72,237 @@
     )
 
 
+MESH_IDS = pl.DeviceIdType.MESH
+
+
+def exchange(name, collective_id, sizes, ops):
+    axes = tuple(dict.fromkeys(op[1] for op in ops))
+    out_shapes = []
+    scratch = []
+    total = 0
+    for array, axis, kind, dim, rolled in ops:
+        n = sizes[axis]
+        shape = list(array.shape)
+        if kind == "gather":
+            shape[dim] *= n
+            out_shapes.append(jax.ShapeDtypeStruct(tuple(shape), array.dtype))
+        else:
+            shape[dim] //= n
+            scratch.append(pltpu.VMEM((n, *shape), array.dtype))
+            if kind == "scatter":
+                out_shapes.append(jax.ShapeDtypeStruct(tuple(shape), jnp.float32))
+            else:
+                out_shapes.append(jax.ShapeDtypeStruct(array.shape, array.dtype))
+        total += array.size
+    n_max = max(sizes[a] for a in axes)
+    count = len(ops)
+    n_scratch = len(scratch)
+
+    def kernel(*refs):
+        ins = refs[:count]
+        outs = refs[count : 2 * count]
+        bufs = list(refs[2 * count : 2 * count + n_scratch])
+        send_sem, recv_sem = refs[2 * count + n_scratch :]
+        barrier = pltpu.get_barrier_semaphore()
+        n_peers = 0
+        for axis in axes:
+            n = sizes[axis]
+            me = lax.axis_index(axis)
+            for k in range(1, n):
+                pl.semaphore_signal(
+                    barrier, inc=1, device_id={axis: lax.rem(me + k, n)}, device_id_type=MESH_IDS
+                )
+                n_peers += 1
+        pl.semaphore_wait(barrier, n_peers)
+
+        def place(ref, index, axis, dim, width, rolled):
+            n = sizes[axis]
+            if rolled:
+                index = lax.rem(index + lax.axis_index("shard") * (n // 2), n)
+            start = pl.multiple_of(index * width, width)
+            if dim == 0:
+                return ref.at[pl.ds(start, width), :]
+            return ref.at[:, pl.ds(start, width)]
+
+        sends = []
+        first = []
+        buf_of = {}
+        for i, (array, axis, kind, dim, rolled) in enumerate(ops):
+            n = sizes[axis]
+            me = lax.axis_index(axis)
+            if kind != "gather":
+                buf_of[i] = bufs.pop(0)
+            for k in range(1, n):
+                peer = lax.rem(me + k, n)
+                source = lax.rem(me - k + n, n)
+                if kind == "gather":
+                    width = array.shape[dim]
+                    src = ins[i]
+                    dst = place(outs[i], me, axis, dim, width, rolled)
+                    land = place(outs[i], source, axis, dim, width, rolled)
+                else:
+                    width = array.shape[dim] // n
+                    src = place(ins[i], peer, axis, dim, width, rolled)
+                    dst = buf_of[i].at[k]
+                    land = dst
+                make = partial(
+                    pltpu.make_async_remote_copy,
+                    src_ref=src,
+                    send_sem=send_sem.at[0, i, k],
+                    recv_sem=recv_sem.at[0, i, k],
+                    device_id={axis: peer},
+                    device_id_type=MESH_IDS,
+                )
+                copy = make(dst_ref=dst)
+                copy.start()
+                sends.append(copy)
+                first.append((i, make(dst_ref=land)))
+        for i, (array, axis, kind, dim, rolled) in enumerate(ops):
+            if kind == "gather":
+                me = lax.axis_index(axis)
+                place(outs[i], me, axis, dim, array.shape[dim], rolled)[...] = ins[i][...]
+        second = []
+        for i, (array, axis, kind, dim, rolled) in enumerate(ops):
+            for j, copy in first:
+                if i == j:
+                    copy.wait_recv()
+            if kind == "gather":
+                continue
+            n = sizes[axis]
+            me = lax.axis_index(axis)
+            width = array.shape[dim] // n
+            summed = place(ins[i], me, axis, dim, width, rolled)[...].astype(jnp.float32)
+            for k in range(1, n):
+                summed = summed + buf_of[i][k].astype(jnp.float32)
+            if kind == "scatter":
+                outs[i][...] = summed
+                continue
+            mine = place(outs[i], me, axis, dim, width, rolled)
+            mine[...] = summed.astype(array.dtype)
+            for k in range(1, n):
+                peer = lax.rem(me + k, n)
+                source = lax.rem(me - k + n, n)
+                make = partial(
+                    pltpu.make_async_remote_copy,
+                    src_ref=mine,
+                    send_sem=send_sem.at[1, i, k],
+                    recv_sem=recv_sem.at[1, i, k],
+                    device_id={axis: peer},
+                    device_id_type=MESH_IDS,
+                )
+                copy = make(dst_ref=mine)
+                copy.start()
+                sends.append(copy)
+                second.append(
+                    make(dst_ref=place(outs[i], source, axis, dim, width, rolled))
+                )
+        for copy in second:
+            copy.wait_recv()
+        for copy in sends:
+            copy.wait_send()
+
+    return pl.pallas_call(
+        kernel,
+        name=name,
+        out_shape=tuple(out_shapes),
+        in_specs=[pl.BlockSpec(memory_space=pltpu.VMEM)] * count,
+        out_specs=tuple([pl.BlockSpec(memory_space=pltpu.VMEM)] * count),
+        scratch_shapes=scratch
+        + [
+            pltpu.SemaphoreType.DMA((2, count, n_max)),
+            pltpu.SemaphoreType.DMA((2, count, n_max)),
+        ],
+        compiler_params=pltpu.CompilerParams(
+            collective_id=collective_id, has_side_effects=True, vmem_limit_bytes=24 * 1024 * 1024
+        ),
+        cost_estimate=pl.CostEstimate(flops=0, bytes_accessed=8 * total, transcendentals=0),
+    )(*[op[0] for op in ops])
+
+
+def total_small(array, sizes):
+    axes = ("tp", "ctx", "shard")
+    n_max = max(sizes[axis] for axis in axes)
+
+    def kernel(in_ref, out_ref, sent, slots, send_sem, recv_sem):
+        barrier = pltpu.get_barrier_semaphore()
+        n_peers = 0
+        for axis in axes:
+            n = sizes[axis]
+            me = lax.axis_index(axis)
+            for k in range(1, n):
+                pl.semaphore_signal(
+                    barrier, inc=1, device_id={axis: lax.rem(me + k, n)}, device_id_type=MESH_IDS
+                )
+                n_peers += 1
+        pl.semaphore_wait(barrier, n_peers)
+        summed = in_ref[...]
+        copies = []
+        for stage, axis in enumerate(axes):
+            n = sizes[axis]
+            me = lax.axis_index(axis)
+            sent[stage] = summed
+            slots[stage, me] = summed
+            here = []
+            for k in range(1, n):
+                make = partial(
+                    pltpu.make_async_remote_copy,
+                    src_ref=sent.at[stage],
+                    send_sem=send_sem.at[stage, k],
+                    recv_sem=recv_sem.at[stage, k],
+                    device_id={axis: lax.rem(me + k, n)},
+                    device_id_type=MESH_IDS,
+                )
+                copy = make(dst_ref=slots.at[stage, me])
+                copy.start()
+                copies.append(copy)
+                here.append(make(dst_ref=slots.at[stage, lax.rem(me - k + n, n)]))
+            for copy in here:
+                copy.wait_recv()
+            summed = slots[stage, 0]
+            for k in range(1, n):
+                summed = summed + slots[stage, k]
+        for copy in copies:
+            copy.wait_send()
+        out_ref[...] = summed
+
+    return pl.pallas_call(
+        kernel,
+        name="sum_gain_gradients",
+        out_shape=jax.ShapeDtypeStruct(array.shape, jnp.float32),
+        in_specs=[pl.BlockSpec(memory_space=pltpu.VMEM)],
+        out_specs=pl.BlockSpec(memory_space=pltpu.VMEM),
+        scratch_shapes=[
+            pltpu.VMEM((len(axes), *array.shape), jnp.float32),
+            pltpu.VMEM((len(axes), n_max, *array.shape), jnp.float32),
+            pltpu.SemaphoreType.DMA((len(axes), n_max)),
+            pltpu.SemaphoreType.DMA((len(axes), n_max)),
+        ],
+        compiler_params=pltpu.CompilerParams(collective_id=6, has_side_effects=True),
+    )(array)
+
+
+def partner(array):
+    return lax.ppermute(array, "shard", [(0, 1), (1, 0)])
+
+
+def grad_shard(grad, dim, n_ctx):
+    half = grad.shape[dim] // 2
+    low = grad.astype(jnp.bfloat16)
+    own = lax.slice_in_dim(low, 0, half, axis=dim)
+    theirs = partner(lax.slice_in_dim(low, half, 2 * half, axis=dim))
+    both = (own.astype(jnp.float32) + theirs.astype(jnp.float32)).astype(jnp.bfloat16)
+    width = half // n_ctx
+    me = lax.axis_index("ctx")
+    total = lax.dynamic_slice_in_dim(both, me * width, width, dim).astype(jnp.float32)
+    for k in range(1, n_ctx):
+        piece = lax.dynamic_slice_in_dim(both, (me ^ k) * width, width, dim)
+        came = lax.ppermute(piece, "ctx", [(i, i ^ k) for i in range(n_ctx)])
+        total = total + came.astype(jnp.float32)
+    return total
+
+
 def body(
+    sizes,
     inputs,
     w_query,
     key_weight,
@@ -85,42 +317,46 @@
     gain_key,
     cotangent,
 ):
-    (
-        w_query,
-        key_weight,
-        value_weight,
-        w_out,
-        w_gate,
-        w_up,
-        w_down,
-        norm_attn,
-        norm_mlp,
-        gain_query,
-        gain_key,
-    ) = (
-        lax.all_gather(w_query, "shard", axis=0, tiled=True),
-        lax.all_gather(key_weight, "shard", axis=0, tiled=True),
-        lax.all_gather(value_weight, "shard", axis=0, tiled=True),
-        lax.all_gather(w_out, "shard", axis=1, tiled=True),
-        lax.all_gather(w_gate, "shard", axis=0, tiled=True),
-        lax.all_gather(w_up, "shard", axis=0, tiled=True),
-        lax.all_gather(w_down, "shard", axis=1, tiled=True),
-        lax.all_gather(norm_attn, "shard", axis=0, tiled=True),
-        lax.all_gather(norm_mlp, "shard", axis=0, tiled=True),
-        lax.all_gather(gain_query, "shard", axis=0, tiled=True),
-        lax.all_gather(gain_key, "shard", axis=0, tiled=True),
-    )
-    norm_attn = norm_attn.astype(jnp.float32)
-    norm_mlp = norm_mlp.astype(jnp.float32)
-    gain_query = gain_query.astype(jnp.float32)
-    gain_key = gain_key.astype(jnp.float32)
+    n_ctx = sizes["ctx"]
+    n_tp = sizes["tp"]
+    shard_index = lax.axis_index("shard")
+    w_query = jnp.concatenate([w_query, partner(w_query)], axis=0)
+    key_weight = jnp.concatenate([key_weight, partner(key_weight)], axis=0)
+    value_weight = jnp.concatenate([value_weight, partner(value_weight)], axis=0)
+    w_out = jnp.concatenate([w_out, partner(w_out)], axis=1)
+    w_gate = jnp.concatenate([w_gate, partner(w_gate)], axis=0)
+    w_up = jnp.concatenate([w_up, partner(w_up)], axis=0)
+    w_down = jnp.concatenate([w_down, partner(w_down)], axis=1)
+    width_half = norm_attn.shape[0]
+    packed = jnp.concatenate([norm_attn, norm_mlp, gain_query, gain_key]).reshape(-1, HEAD_SIZE)
+    pack_rows = packed.shape[0]
+    packed = jnp.pad(packed, ((0, -pack_rows % 16), (0, 0)))
     local_tokens = inputs.shape[1]
     width_part = inputs.shape[2]
-    feature_start = lax.axis_index("tp") * width_part
     offset = lax.axis_index("ctx") * local_tokens
     query_pos = offset + jnp.arange(local_tokens, dtype=jnp.int32)
     positions = query_pos.astype(jnp.float32)
-    full_in = lax.all_gather(inputs, "tp", axis=2, tiled=True).reshape(local_tokens, -1)
+    full_in, gains = exchange(
+        "gather_inputs",
+        0,
+        sizes,
+        [
+            (inputs.reshape(local_tokens, width_part), "tp", "gather", 1, True),
+            (packed, "shard", "gather", 0, False),
+        ],
+    )
+    gains = gains.reshape(2, -1).astype(jnp.float32)
+    own_gains = jnp.where(shard_index == 0, gains[0], gains[1])
+    other_gains = jnp.where(shard_index == 0, gains[1], gains[0])
+    norm_attn = jnp.concatenate([own_gains[:width_half], other_gains[:width_half]])
+    norm_mlp = jnp.concatenate(
+        [own_gains[width_half : 2 * width_half], other_gains[width_half : 2 * width_half]]
+    )
+    small = 2 * width_half
+    part = HEAD_SIZE // 2
+    gain_query = gains[:, small : small + part].reshape(-1)
+    gain_key = gains[:, small + part : small + 2 * part].reshape(-1)
+    feature_start = lax.rem(lax.axis_index("tp") + shard_index * (n_tp // 2), n_tp) * width_part
     resid_in = full_in.astype(jnp.float32)
     normed_low = rms_norm(resid_in, norm_attn).astype(jnp.bfloat16)
     query_proj = jnp.dot(normed_low, w_query, preferred_element_type=jnp.float32)
@@ -132,9 +368,15 @@
     query_low = query_heads.astype(jnp.bfloat16)
     key_low = key_heads.astype(jnp.bfloat16)
     value_low = value_proj.astype(jnp.bfloat16)
-    key_all, value_all = (
-        lax.all_gather(key_low, "ctx", axis=0, tiled=True),
-        lax.all_gather(value_low, "ctx", axis=0, tiled=True),
+    key_all, value_all, grad_out = exchange(
+        "gather_keys_values",
+        1,
+        sizes,
+        [
+            (key_low, "ctx", "gather", 0, False),
+            (value_low, "ctx", "gather", 0, False),
+            (cotangent.reshape(local_tokens, width_part), "tp", "gather", 1, True),
+        ],
     )
     kv_local = key_low.shape[1] // HEAD_SIZE
     heads_per_group = query_low.shape[1] // (HEAD_SIZE * kv_local)
@@ -168,19 +410,14 @@
         row_totals.append(row_total)
     attended_low = jnp.concatenate(attended_parts, axis=1).astype(jnp.bfloat16)
     attn_part = jnp.dot(attended_low, w_out, preferred_element_type=jnp.float32)
-    mixed = resid_in + lax.psum(attn_part.astype(jnp.bfloat16), "tp").astype(jnp.float32)
+    mixed = resid_in + exchange(
+        "sum_attention", 2, sizes, [(attn_part.astype(jnp.bfloat16), "tp", "reduce", 1, True)]
+    )[0].astype(jnp.float32)
     normed_mlp_low = rms_norm(mixed, norm_mlp).astype(jnp.bfloat16)
     gate_act = jnp.dot(normed_mlp_low, w_gate, preferred_element_type=jnp.float32)
     up_act = jnp.dot(normed_mlp_low, w_up, preferred_element_type=jnp.float32)
     hidden_low = (jax.nn.silu(gate_act) * up_act).astype(jnp.bfloat16)
     mlp_part = jnp.dot(hidden_low, w_down, preferred_element_type=jnp.float32)
-    result = mixed + lax.psum(mlp_part.astype(jnp.bfloat16), "tp").astype(jnp.float32)
-    outputs = (
-        lax.dynamic_slice_in_dim(result, feature_start, width_part, 1)
-        .astype(jnp.bfloat16)
-        .reshape(1, local_tokens, width_part)
-    )
-    grad_out = lax.all_gather(cotangent, "tp", axis=2, tiled=True).reshape(local_tokens, -1)
     d_down = jnp.einsum("tf,td->fd", hidden_low, grad_out, preferred_element_type=jnp.float32)
     d_hidden = jnp.einsum("td,fd->tf", grad_out, w_down, preferred_element_type=jnp.float32)
     sigmoid_gate = jax.nn.sigmoid(gate_act)
@@ -194,7 +431,21 @@
     d_normed_mlp = d_normed_mlp + jnp.einsum(
         "tf,df->td", d_up_low, w_up, preferred_element_type=jnp.float32
     )
-    d_normed_mlp = lax.psum(d_normed_mlp.astype(jnp.bfloat16), "tp").astype(jnp.float32)
+    mlp_sum, d_normed_mlp = exchange(
+        "sum_feed_forward",
+        3,
+        sizes,
+        [
+            (mlp_part.astype(jnp.bfloat16), "tp", "scatter", 1, True),
+            (d_normed_mlp.astype(jnp.bfloat16), "tp", "reduce", 1, True),
+        ],
+    )
+    d_normed_mlp = d_normed_mlp.astype(jnp.float32)
+    outputs = (
+        (lax.dynamic_slice_in_dim(mixed, feature_start, width_part, 1) + mlp_sum)
+        .astype(jnp.bfloat16)
+        .reshape(1, local_tokens, width_part)
+    )
     d_mix_norm, d_norm_mlp = rms_back(mixed, norm_mlp, d_normed_mlp)
     d_mixed = grad_out.astype(jnp.float32) + d_mix_norm
     d_mixed_low = d_mixed.astype(jnp.bfloat16)
@@ -226,13 +477,14 @@
     d_query_heads = jnp.concatenate(d_query_parts, axis=1)
     d_keys_all = jnp.concatenate(d_key_parts, axis=1)
     d_values_all = jnp.concatenate(d_value_parts, axis=1)
-    d_key_heads, d_value_proj = (
-        lax.psum_scatter(
-            d_keys_all.astype(jnp.bfloat16), "ctx", scatter_dimension=0, tiled=True
-        ).astype(jnp.float32),
-        lax.psum_scatter(
-            d_values_all.astype(jnp.bfloat16), "ctx", scatter_dimension=0, tiled=True
-        ).astype(jnp.float32),
+    d_key_heads, d_value_proj = exchange(
+        "sum_keys_values",
+        4,
+        sizes,
+        [
+            (d_keys_all.astype(jnp.bfloat16), "ctx", "scatter", 0, False),
+            (d_values_all.astype(jnp.bfloat16), "ctx", "scatter", 0, False),
+        ],
     )
     d_query_proj, d_gain_query = query_pull(d_query_heads)
     d_key_proj, d_gain_key = key_pull(d_key_heads)
@@ -249,11 +501,9 @@
     d_normed = d_normed + jnp.einsum(
         "th,dh->td", d_value_low, value_weight, preferred_element_type=jnp.float32
     )
-    d_normed, d_gain_query, d_gain_key = (
-        lax.psum(d_normed.astype(jnp.bfloat16), "tp").astype(jnp.float32),
-        lax.psum(d_gain_query.astype(jnp.bfloat16), "tp").astype(jnp.float32),
-        lax.psum(d_gain_key.astype(jnp.bfloat16), "tp").astype(jnp.float32),
-    )
+    d_normed = exchange(
+        "sum_input_gradient", 5, sizes, [(d_normed.astype(jnp.bfloat16), "tp", "reduce", 1, True)]
+    )[0].astype(jnp.float32)
     d_in_norm, d_norm_attn = rms_back(resid_in, norm_attn, d_normed)
     d_full = d_mixed + d_in_norm
     d_inputs = (
@@ -261,60 +511,40 @@
         .astype(jnp.bfloat16)
         .reshape(1, local_tokens, width_part)
     )
+    norms = jnp.stack([d_norm_attn, d_norm_mlp]).reshape(2, 2, width_half) * (1.0 / n_tp)
+    norms = jnp.where(shard_index == 0, norms, norms[:, ::-1]).reshape(-1)
+    small = jnp.concatenate([norms, d_gain_query, d_gain_key]).reshape(-1, HEAD_SIZE)
+    small = jnp.pad(small, ((0, -small.shape[0] % 8), (0, 0)))
+    small = total_small(small, sizes)
+    small = small.reshape(-1)
+    place = shard_index * n_ctx + lax.axis_index("ctx")
+    full_width = 2 * width_half
+    ranks = 2 * n_ctx
+
+    def own_part(start, size):
+        return lax.dynamic_slice_in_dim(
+            small[start : start + size], place * (size // ranks), size // ranks, 0
+        )
+
     gradients = (
-        d_query,
-        d_key,
-        d_value,
-        d_out,
-        d_gate,
-        d_up,
-        d_down,
-        d_norm_attn,
-        d_norm_mlp,
-        d_gain_query,
-        d_gain_key,
-    )
-    gradients = (
-        lax.psum_scatter(
-            d_query.astype(jnp.bfloat16), ("shard", "ctx"), scatter_dimension=0, tiled=True
-        ).astype(jnp.float32),
-        lax.psum_scatter(
-            d_key.astype(jnp.bfloat16), ("shard", "ctx"), scatter_dimension=0, tiled=True
-        ).astype(jnp.float32),
-        lax.psum_scatter(
-            d_value.astype(jnp.bfloat16), ("shard", "ctx"), scatter_dimension=0, tiled=True
-        ).astype(jnp.float32),
-        lax.psum_scatter(
-            d_out.astype(jnp.bfloat16), ("shard", "ctx"), scatter_dimension=1, tiled=True
-        ).astype(jnp.float32),
-        lax.psum_scatter(
-            d_gate.astype(jnp.bfloat16), ("shard", "ctx"), scatter_dimension=0, tiled=True
-        ).astype(jnp.float32),
-        lax.psum_scatter(
-            d_up.astype(jnp.bfloat16), ("shard", "ctx"), scatter_dimension=0, tiled=True
-        ).astype(jnp.float32),
-        lax.psum_scatter(
-            d_down.astype(jnp.bfloat16), ("shard", "ctx"), scatter_dimension=1, tiled=True
-        ).astype(jnp.float32),
-        lax.psum_scatter(
-            d_norm_attn.astype(jnp.bfloat16), ("shard", "ctx"), scatter_dimension=0, tiled=True
-        ).astype(jnp.float32),
-        lax.psum_scatter(
-            d_norm_mlp.astype(jnp.bfloat16), ("shard", "ctx"), scatter_dimension=0, tiled=True
-        ).astype(jnp.float32),
-        lax.psum_scatter(
-            d_gain_query.astype(jnp.bfloat16), ("shard", "ctx"), scatter_dimension=0, tiled=True
-        ).astype(jnp.float32),
-        lax.psum_scatter(
-            d_gain_key.astype(jnp.bfloat16), ("shard", "ctx"), scatter_dimension=0, tiled=True
-        ).astype(jnp.float32),
+        grad_shard(d_query, 0, n_ctx),
+        grad_shard(d_key, 0, n_ctx),
+        grad_shard(d_value, 0, n_ctx),
+        grad_shard(d_out, 1, n_ctx),
+        grad_shard(d_gate, 0, n_ctx),
+        grad_shard(d_up, 0, n_ctx),
+        grad_shard(d_down, 1, n_ctx),
+        own_part(0, full_width),
+        own_part(full_width, full_width),
+        own_part(2 * full_width, HEAD_SIZE),
+        own_part(2 * full_width + HEAD_SIZE, HEAD_SIZE),
     )
     return (outputs, d_inputs) + tuple(gradients)
 
 
 def solution(mesh):
     return jax.shard_map(
-        body,
+        partial(body, dict(mesh.shape)),
         mesh=mesh,
         in_specs=(
             P("shard", "ctx", "tp"),

time: 638 us -> 313 us (0.49)
  waiting for transfers between devices: 403 us -> 26.6 us
  Pallas kernels: 0 us -> 150 us
  blocking collectives: 101 us -> 0 us
  starting transfers between devices: 0.91 us -> 28.7 us
  matrix products: 47.5 us -> 31.3 us
  between operations: 16.9 us -> 2.31 us
  local copies, waits for them, and re-layouts: 28.2 us -> 42.1 us
  other arithmetic: 39.4 us -> 30.7 us
    reduce_scatter x7 -> x0, waiting for transfers between devices: 205 us -> none  [the longest x1 39.7 us: body(): lax.psum_scatter(d_gate.astype(jnp.bfloat16), ('shard', 'ctx'), scatter_d...]
    pallas_call x0 -> x7, Pallas kernels: none -> 150 us  [the longest x6 136 us: exchange(): pl.pallas_call(kernel, name=name, out_shape=tuple(out_shapes), in_specs=[...]
    psum x3 -> x0, waiting for transfers between devices: 111 us -> none  [the longest x1 52.8 us: body(): lax.psum(mlp_part.astype(jnp.bfloat16), 'tp').astype(jnp.float32)]
    all_gather x8 -> x0, blocking collectives: 72.6 us -> none  [the longest x1 22.8 us: body(): lax.all_gather(cotangent, 'tp', axis=2, tiled=True)]
    unnamed x19 -> x0, waiting for transfers between devices: 59.2 us -> none
    ppermute x0 -> x35, starting transfers between devices: none -> 28.7 us  [the longest x21 25.1 us: grad_shard(): came = lax.ppermute(piece, 'ctx', [(i, i ^ k) for i in range(n_ctx)])]
    all_gather x5 -> x0, waiting for transfers between devices: 27.2 us -> none  [the longest x1 9.54 us: body(): lax.all_gather(w_up, 'shard', axis=0, tiled=True)]
    ppermute x0 -> x35, waiting for transfers between devices: none -> 26.6 us  [the longest x21 26.6 us: grad_shard(): came = lax.ppermute(piece, 'ctx', [(i, i ^ k) for i in range(n_ctx)])]
  transfers between devices with their start and end apart: 17 -> 35, of which waited for: 15 -> 15; matrix products, arithmetic and copies ran while one was open for 12% -> 17% of each run, Pallas kernels for 0% -> 19%
where the time goes in v1:
time: 313 us; the launch traced here: 312 us
  Pallas kernels  150 us (48%)
  local copies, waits for them, and re-layouts  42.1 us (13%)
  matrix products  31.3 us (10%)
  other arithmetic  30.7 us (10%)
  starting transfers between devices  28.7 us (9%)
  waiting for transfers between devices  26.6 us (8%)
    pallas_call x6, Pallas kernels, exchange(): pl.pallas_call(kernel, name=name, out_shape=tuple(out_shapes), in_specs=[...  136 us
    ppermute x21, waiting for transfers between devices, grad_shard(): came = lax.ppermute(piece, 'ctx', [(i, i ^ k) for i in range(n_ctx)])  26.6 us
    ppermute x21, starting transfers between devices, grad_shard(): came = lax.ppermute(piece, 'ctx', [(i, i ^ k) for i in range(n_ctx)])  25.1 us
    unnamed x167, local copies, waits for them, and re-layouts  19.2 us
    pallas_call x1, Pallas kernels, total_small(): pl.pallas_call(kernel, name='sum_gain_gradients', out_shape=jax.ShapeDtyp...  14.8 us
  transfers between devices with their start and end apart: 35, of which 15 were waited for; matrix products, arithmetic and copies ran while one was open for 17% of the time, Pallas kernels for 19%

profile of v1, /device:TPU:0, one launch (start us, length us, event | category | flops | bytes accessed | tf_op | source)
XLA Modules:
  0.0 312.1 jit_solution(8757256975527918004)
XLA Ops:
  4.1 2.8 concatenate.64
  7.9 14.9 %gather_inputs.1 = (bf16[256,1024]{1,0:T(8,128)(2,1)S(1)}, bf16[32,128]{1,0:T(8,128)(2,1)S(1)}) custom-call(bf16[256,256]{1,0:T(8,128)(2,1)S(1)} %bitcast.156, bf16[16,128]{1,0:T(8,128)(2,1)S(1)} %pad.20.refs_1_), custom_call_target="tpu_custom_call" | custom-call | bytes 540672 | tf_op jit(solution)/shard_map/gather_inputs/pallas_call | solution.py:204
  22.9 1.9 constant_dynamic-update-slice_fusion.1
  30.0 2.1 constant_dynamic-update-slice_fusion.13
  37.3 19.1 %gather_keys_values.1 = (bf16[1024,256]{1,0:T(8,128)(2,1)S(1)}, bf16[1024,256]{1,0:T(8,128)(2,1)S(1)}, bf16[256,1024]{1,0:T(8,128)(2,1)S(1)}) custom-call(bf16[256,256]{1,0:T(8,128)(2,1)S(1)} %add_convert_fusion.8.refs_0_, bf16[256,256]{1,0:T(8,128)(2,1)S(1)} %convolution_convert_fusion.12.refs_1_, bf16[256,256]{1,0:T(8,128)(2,1)S(1)} %bitcast.155), custom_call_target="tpu_custom_call" | custom-call | bytes 1572864 | tf_op jit(solution)/shard_map/gather_keys_values/pallas_call | solution.py:204
  56.4 1.9 constant_dynamic-update-slice_fusion
  63.7 2.5 fusion.64
  70.5 2.2 fusion.3
  75.3 2.0 constant_dynamic-update-slice_fusion.6
  79.0 23.8 %sum_attention.1 = bf16[256,1024]{1,0:T(8,128)(2,1)S(1)} custom-call(bf16[256,1024]{1,0:T(8,128)(2,1)S(1)} %convolution_convert_fusion.7.refs_0_), custom_call_target="tpu_custom_call" | custom-call | bytes 2097152 | tf_op jit(solution)/shard_map/sum_attention/pallas_call | solution.py:204
  111.9 36.7 %sum_feed_forward.1 = (f32[256,256]{1,0:T(8,128)S(1)}, bf16[256,1024]{1,0:T(8,128)(2,1)S(1)}) custom-call(bf16[256,1024]{1,0:T(8,128)(2,1)S(1)} %convolution_convert_fusion.8.refs_0_, bf16[256,1024]{1,0:T(8,128)(2,1)S(1)} %fusion.5.refs_1_), custom_call_target="tpu_custom_call" | custom-call | bytes 4194304 | tf_op jit(solution)/shard_map/sum_feed_forward/pallas_call | solution.py:204
  162.1 13.3 %sum_keys_values.1 = (f32[256,256]{1,0:T(8,128)S(1)}, f32[256,256]{1,0:T(8,128)S(1)}) custom-call(bf16[1024,256]{1,0:T(8,128)(2,1)S(1)} %pad_maximum_fusion.1.refs_0_, bf16[1024,256]{1,0:T(8,128)(2,1)S(1)} %pad_maximum_fusion.2.refs_1_), custom_call_target="tpu_custom_call" | custom-call | bytes 4194304 | tf_op jit(solution)/shard_map/sum_keys_values/pallas_call | solution.py:204
  184.8 1.8 convolution_convert_fusion
  195.3 2.2 convolution_convert_fusion.4
  198.1 27.9 %sum_input_gradient.1 = bf16[256,1024]{1,0:T(8,128)(2,1)S(1)} custom-call(bf16[256,1024]{1,0:T(8,128)(2,1)S(1)} %fusion.6.refs_0_), custom_call_target="tpu_custom_call" | custom-call | bytes 2097152 | tf_op jit(solution)/shard_map/sum_input_gradient/pallas_call | solution.py:204
  227.4 14.8 %sum_gain_gradients.1 = f32[24,128]{1,0:T(8,128)} custom-call(f32[24,128]{1,0:T(8,128)} %pad.25.in_ref), custom_call_target="tpu_custom_call" | custom-call | tf_op jit(solution)/shard_map/sum_gain_gradients/pallas_call | solution.py:268
  248.1 1.7 fusion.45
  270.1 2.6 collective-permute-done.8
  274.3 2.2 collective-permute-done.10
  279.3 3.1 collective-permute-done.22
  291.0 1.7 collective-permute-done.32
  293.4 3.7 %collective-permute-done.34 = bf16[768,128]{1,0:T(8,128)(2,1)S(1)} collective-permute-done((bf16[768,128]{1,0:T(8,128)(2,1)S(1)}, bf16[768,128]{1,0:T(8,128)(2,1)S(1)}, u32[]{:S(2)}, u32[]{:S(2)}) %collective-permute-start.34) | collective-permute-done | bytes 196640 | tf_op jit(solution)/shard_map/ppermute | solution.py:299
  302.9 2.7 collective-permute-done.26
  307.9 2.1 collective-permute-done.30
  (386 shorter events, 120.1 us)
Async XLA Ops:
  0.7 32.2 %collective-permute-start.1 = (bf16[512,256]{1,0:T(8,128)(2,1)}, bf16[512,256]{1,0:T(8,128)(2,1)}, u32[]{:S(2)}, u32[]{:S(2)}) collective-permute-start(bf16[512,256]{1,0:T(8,128)(2,1)} %param.15), channel_id=1, source_target_pairs={{0,16},{16,0},{1,17},{17,1},{2,18},{18,2},{3,19},{19,3},{4,20},{20... | collective-permute-start | bytes 786440 | tf_op jit(solution)/shard_map/ppermute | solution.py:285
  1.2 34.0 %collective-permute-start.2 = (bf16[512,256]{1,0:T(8,128)(2,1)}, bf16[512,256]{1,0:T(8,128)(2,1)S(1)}, u32[]{:S(2)}, u32[]{:S(2)}) collective-permute-start(bf16[512,256]{1,0:T(8,128)(2,1)} %param.16), channel_id=1, source_target_pairs={{0,16},{16,0},{1,17},{17,1},{2,18},{18,2},{3,19},{19,3},{4,20},{20... | collective-permute-start | bytes 786440 | tf_op jit(solution)/shard_map/ppermute | solution.py:285
  1.3 55.2 %collective-permute-start = (bf16[512,512]{1,0:T(8,128)(2,1)}, bf16[512,512]{1,0:T(8,128)(2,1)}, u32[]{:S(2)}, u32[]{:S(2)}) collective-permute-start(bf16[512,512]{1,0:T(8,128)(2,1)} %param.14), channel_id=1, source_target_pairs={{0,16},{16,0},{1,17},{17,1},{2,18},{18,2},{3,19},{19,3},{4,20},{20... | collective-permute-start | bytes 1572872 | tf_op jit(solution)/shard_map/ppermute | solution.py:285
  1.7 73.6 %collective-permute-start.3 = (bf16[512,512]{1,0:T(8,128)(2,1)}, bf16[512,512]{1,0:T(8,128)(2,1)}, u32[]{:S(2)}, u32[]{:S(2)}) collective-permute-start(bf16[512,512]{1,0:T(8,128)(2,1)} %param.17), channel_id=1, source_target_pairs={{0,16},{16,0},{1,17},{17,1},{2,18},{18,2},{3,19},{19,3},{4,20},{20... | collective-permute-start | bytes 1572872 | tf_op jit(solution)/shard_map/ppermute | solution.py:285
  1.8 105.4 %collective-permute-start.4 = (bf16[512,768]{1,0:T(8,128)(2,1)}, bf16[512,768]{1,0:T(8,128)(2,1)}, u32[]{:S(2)}, u32[]{:S(2)}) collective-permute-start(bf16[512,768]{1,0:T(8,128)(2,1)} %param.18), channel_id=1, source_target_pairs={{0,16},{16,0},{1,17},{17,1},{2,18},{18,2},{3,19},{19,3},{4,20},{20... | collective-permute-start | bytes 2359304 | tf_op jit(solution)/shard_map/ppermute | solution.py:285
  32.8 70.4 %collective-permute-start.5 = (bf16[512,768]{1,0:T(8,128)(2,1)}, bf16[512,768]{1,0:T(8,128)(2,1)}, u32[]{:S(2)}, u32[]{:S(2)}) collective-permute-start(bf16[512,768]{1,0:T(8,128)(2,1)} %param.19), channel_id=1, source_target_pairs={{0,16},{16,0},{1,17},{17,1},{2,18},{18,2},{3,19},{19,3},{4,20},{20... | collective-permute-start | bytes 2359304 | tf_op jit(solution)/shard_map/ppermute | solution.py:285
  35.1 69.4 %collective-permute-start.6 = (bf16[768,512]{1,0:T(8,128)(2,1)}, bf16[768,512]{1,0:T(8,128)(2,1)}, u32[]{:S(2)}, u32[]{:S(2)}) collective-permute-start(bf16[768,512]{1,0:T(8,128)(2,1)} %param.20), channel_id=1, source_target_pairs={{0,16},{16,0},{1,17},{17,1},{2,18},{18,2},{3,19},{19,3},{4,20},{20... | collective-permute-start | bytes 2359304 | tf_op jit(solution)/shard_map/ppermute | solution.py:285
  246.5 9.3 %collective-permute-start.15 = (bf16[512,256]{1,0:T(8,128)(2,1)S(1)}, bf16[512,256]{1,0:T(8,128)(2,1)S(1)}, u32[]{:S(2)}, u32[]{:S(2)}) collective-permute-start(bf16[512,256]{1,0:T(8,128)(2,1)S(1)} %slice.209), channel_id=1, source_target_pairs={{0,16},{16,0},{1,17},{17,1},{2,18},{18,2},{3,19},{19,3},{4,20},{20... | collective-permute-start | bytes 786440 | tf_op jit(solution)/shard_map/ppermute | solution.py:285
  246.9 19.2 %collective-permute-start.7 = (bf16[512,512]{1,0:T(8,128)(2,1)S(1)}, bf16[512,512]{1,0:T(8,128)(2,1)S(1)}, u32[]{:S(2)}, u32[]{:S(2)}) collective-permute-start(bf16[512,512]{1,0:T(8,128)(2,1)S(1)} %slice.205), channel_id=1, source_target_pairs={{0,16},{16,0},{1,17},{17,1},{2,18},{18,2},{3,19},{19,3},{4,20},{20... | collective-permute-start | bytes 1572872 | tf_op jit(solution)/shard_map/ppermute | solution.py:285
  247.2 22.0 %collective-permute-start.19 = (bf16[512,512]{1,0:T(8,128)(2,1)S(1)}, bf16[512,512]{1,0:T(8,128)(2,1)S(1)}, u32[]{:S(2)}, u32[]{:S(2)}) collective-permute-start(bf16[512,512]{1,0:T(8,128)(2,1)S(1)} %slice.211), channel_id=1, source_target_pairs={{0,16},{16,0},{1,17},{17,1},{2,18},{18,2},{3,19},{19,3},{4,20},{20... | collective-permute-start | bytes 1572872 | tf_op jit(solution)/shard_map/ppermute | solution.py:285
  263.1 21.3 %collective-permute-start.31 = (bf16[768,512]{1,0:T(8,128)(2,1)S(1)}, bf16[768,512]{1,0:T(8,128)(2,1)S(1)}, u32[]{:S(2)}, u32[]{:S(2)}) collective-permute-start(bf16[768,512]{1,0:T(8,128)(2,1)S(1)} %slice.217), channel_id=1, source_target_pairs={{0,16},{16,0},{1,17},{17,1},{2,18},{18,2},{3,19},{19,3},{4,20},{20... | collective-permute-start | bytes 2359304 | tf_op jit(solution)/shard_map/ppermute | solution.py:285
  264.7 23.7 %collective-permute-start.23 = (bf16[512,768]{1,0:T(8,128)(2,1)S(1)}, bf16[512,768]{1,0:T(8,128)(2,1)S(1)}, u32[]{:S(2)}, u32[]{:S(2)}) collective-permute-start(bf16[512,768]{1,0:T(8,128)(2,1)S(1)} %slice.213), channel_id=1, source_target_pairs={{0,16},{16,0},{1,17},{17,1},{2,18},{18,2},{3,19},{19,3},{4,20},{20... | collective-permute-start | bytes 2359304 | tf_op jit(solution)/shard_map/ppermute | solution.py:285
  267.9 8.5 %collective-permute-start.10 = (bf16[128,512]{1,0:T(8,128)(2,1)S(1)}, bf16[128,512]{1,0:T(8,128)(2,1)S(1)}, u32[]{:S(2)}, u32[]{:S(2)}) collective-permute-start(bf16[128,512]{1,0:T(8,128)(2,1)S(1)} %get-tuple-element.61), channel_id=1, source_target_pairs={{0,12},{4,8},{8,4},{12,0},{1,13},{5,9},{9,5},{13,1},{2,14},{6,10},... | collective-permute-start | bytes 393224 | tf_op jit(solution)/shard_map/ppermute | solution.py:299
  269.2 8.7 %collective-permute-start.9 = (bf16[128,512]{1,0:T(8,128)(2,1)S(1)}, bf16[128,512]{1,0:T(8,128)(2,1)S(1)}, u32[]{:S(2)}, u32[]{:S(2)}) collective-permute-start(bf16[128,512]{1,0:T(8,128)(2,1)S(1)} %get-tuple-element.62), channel_id=1, source_target_pairs={{0,8},{4,12},{8,0},{12,4},{1,9},{5,13},{9,1},{13,5},{2,10},{6,14},... | collective-permute-start | bytes 393224 | tf_op jit(solution)/shard_map/ppermute | solution.py:299
  279.3 10.1 %collective-permute-start.27 = (bf16[512,768]{1,0:T(8,128)(2,1)S(1)}, bf16[512,768]{1,0:T(8,128)(2,1)S(1)}, u32[]{:S(2)}, u32[]{:S(2)}) collective-permute-start(bf16[512,768]{1,0:T(8,128)(2,1)S(1)} %slice.215), channel_id=1, source_target_pairs={{0,16},{16,0},{1,17},{17,1},{2,18},{18,2},{3,19},{19,3},{4,20},{20... | collective-permute-start | bytes 2359304 | tf_op jit(solution)/shard_map/ppermute | solution.py:285
  284.8 7.9 %collective-permute-start.32 = (bf16[768,128]{1,0:T(8,128)(2,1)S(1)}, bf16[768,128]{1,0:T(8,128)(2,1)S(1)}, u32[]{:S(2)}, u32[]{:S(2)}) collective-permute-start(bf16[768,128]{1,0:T(8,128)(2,1)S(1)} %get-tuple-element.46), channel_id=1, source_target_pairs={{0,4},{4,0},{8,12},{12,8},{1,5},{5,1},{9,13},{13,9},{2,6},{6,2},{1... | collective-permute-start | bytes 589832 | tf_op jit(solution)/shard_map/ppermute | solution.py:299
  285.5 11.6 %collective-permute-start.34 = (bf16[768,128]{1,0:T(8,128)(2,1)S(1)}, bf16[768,128]{1,0:T(8,128)(2,1)S(1)}, u32[]{:S(2)}, u32[]{:S(2)}) collective-permute-start(bf16[768,128]{1,0:T(8,128)(2,1)S(1)} %get-tuple-element.47), channel_id=1, source_target_pairs={{0,12},{4,8},{8,4},{12,0},{1,13},{5,9},{9,5},{13,1},{2,14},{6,10},... | collective-permute-start | bytes 589832 | tf_op jit(solution)/shard_map/ppermute | solution.py:299
  287.0 12.1 %collective-permute-start.33 = (bf16[768,128]{1,0:T(8,128)(2,1)S(1)}, bf16[768,128]{1,0:T(8,128)(2,1)S(1)}, u32[]{:S(2)}, u32[]{:S(2)}) collective-permute-start(bf16[768,128]{1,0:T(8,128)(2,1)S(1)} %get-tuple-element.48), channel_id=1, source_target_pairs={{0,8},{4,12},{8,0},{12,4},{1,9},{5,13},{9,1},{13,5},{2,10},{6,14},... | collective-permute-start | bytes 589832 | tf_op jit(solution)/shard_map/ppermute | solution.py:299
  288.6 12.7 %collective-permute-start.24 = (bf16[128,768]{1,0:T(8,128)(2,1)S(1)}, bf16[128,768]{1,0:T(8,128)(2,1)S(1)}, u32[]{:S(2)}, u32[]{:S(2)}) collective-permute-start(bf16[128,768]{1,0:T(8,128)(2,1)S(1)} %get-tuple-element.52), channel_id=1, source_target_pairs={{0,4},{4,0},{8,12},{12,8},{1,5},{5,1},{9,13},{13,9},{2,6},{6,2},{1... | collective-permute-start | bytes 589832 | tf_op jit(solution)/shard_map/ppermute | solution.py:299
  289.3 16.3 %collective-permute-start.26 = (bf16[128,768]{1,0:T(8,128)(2,1)S(1)}, bf16[128,768]{1,0:T(8,128)(2,1)S(1)}, u32[]{:S(2)}, u32[]{:S(2)}) collective-permute-start(bf16[128,768]{1,0:T(8,128)(2,1)S(1)} %get-tuple-element.53), channel_id=1, source_target_pairs={{0,12},{4,8},{8,4},{12,0},{1,13},{5,9},{9,5},{13,1},{2,14},{6,10},... | collective-permute-start | bytes 589832 | tf_op jit(solution)/shard_map/ppermute | solution.py:299
  292.8 14.3 %collective-permute-start.25 = (bf16[128,768]{1,0:T(8,128)(2,1)S(1)}, bf16[128,768]{1,0:T(8,128)(2,1)S(1)}, u32[]{:S(2)}, u32[]{:S(2)}) collective-permute-start(bf16[128,768]{1,0:T(8,128)(2,1)S(1)} %get-tuple-element.54), channel_id=1, source_target_pairs={{0,8},{4,12},{8,0},{12,4},{1,9},{5,13},{9,1},{13,5},{2,10},{6,14},... | collective-permute-start | bytes 589832 | tf_op jit(solution)/shard_map/ppermute | solution.py:299
  297.1 10.8 %collective-permute-start.28 = (bf16[128,768]{1,0:T(8,128)(2,1)S(1)}, bf16[128,768]{1,0:T(8,128)(2,1)S(1)}, u32[]{:S(2)}, u32[]{:S(2)}) collective-permute-start(bf16[128,768]{1,0:T(8,128)(2,1)S(1)} %get-tuple-element.49), channel_id=1, source_target_pairs={{0,4},{4,0},{8,12},{12,8},{1,5},{5,1},{9,13},{13,9},{2,6},{6,2},{1... | collective-permute-start | bytes 589832 | tf_op jit(solution)/shard_map/ppermute | solution.py:299
  299.0 11.0 %collective-permute-start.30 = (bf16[128,768]{1,0:T(8,128)(2,1)S(1)}, bf16[128,768]{1,0:T(8,128)(2,1)S(1)}, u32[]{:S(2)}, u32[]{:S(2)}) collective-permute-start(bf16[128,768]{1,0:T(8,128)(2,1)S(1)} %get-tuple-element.50), channel_id=1, source_target_pairs={{0,12},{4,8},{8,4},{12,0},{1,13},{5,9},{9,5},{13,1},{2,14},{6,10},... | collective-permute-start | bytes 589832 | tf_op jit(solution)/shard_map/ppermute | solution.py:299
  301.3 10.0 %collective-permute-start.29 = (bf16[128,768]{1,0:T(8,128)(2,1)S(1)}, bf16[128,768]{1,0:T(8,128)(2,1)S(1)}, u32[]{:S(2)}, u32[]{:S(2)}) collective-permute-start(bf16[128,768]{1,0:T(8,128)(2,1)S(1)} %get-tuple-element.51), channel_id=1, source_target_pairs={{0,8},{4,12},{8,0},{12,4},{1,9},{5,13},{9,1},{13,5},{2,10},{6,14},... | collective-permute-start | bytes 589832 | tf_op jit(solution)/shard_map/ppermute | solution.py:299
  (89 other events, 505.7 us)

commit v2 on v1

--- a/solution.py
+++ b/solution.py
@@ -76,33 +76,52 @@
 
 
 def exchange(name, collective_id, sizes, ops):
-    axes = tuple(dict.fromkeys(op[1] for op in ops))
+    axes = []
     out_shapes = []
     scratch = []
+    slots_of = []
     total = 0
-    for array, axis, kind, dim, rolled in ops:
-        n = sizes[axis]
+    n_sems = 0
+    for array, op_axes, kind, dim in ops:
+        axes += op_axes
         shape = list(array.shape)
+        slots_of.append(len(scratch))
+        total += array.size
+        n = sizes[op_axes[0]]
+        dtype = array.dtype
         if kind == "gather":
             shape[dim] *= n
-            out_shapes.append(jax.ShapeDtypeStruct(tuple(shape), array.dtype))
+            n_sems += n
+        elif kind == "scatter":
+            shape[dim] //= n
+            scratch.append(pltpu.VMEM((n, *shape), dtype))
+            dtype = jnp.float32
+            n_sems += n
+        elif kind == "reduce":
+            scratch.append(pltpu.VMEM((n, shape[0], shape[1] // n), dtype))
+            n_sems += 2 * n
+        elif kind == "grad":
+            half = shape[0] // 2
+            scratch.append(pltpu.VMEM((half, shape[1]), dtype))
+            scratch.append(pltpu.VMEM((half, shape[1]), dtype))
+            shape[0] = half // sizes["ctx"]
+            scratch.append(pltpu.VMEM((sizes["ctx"], *shape), dtype))
+            dtype = jnp.float32
+            n_sems += 1 + sizes["ctx"]
         else:
-            shape[dim] //= n
-            scratch.append(pltpu.VMEM((n, *shape), array.dtype))
-            if kind == "scatter":
-                out_shapes.append(jax.ShapeDtypeStruct(tuple(shape), jnp.float32))
-            else:
-                out_shapes.append(jax.ShapeDtypeStruct(array.shape, array.dtype))
-        total += array.size
-    n_max = max(sizes[a] for a in axes)
+            n_max = max(sizes[axis] for axis in op_axes)
+            scratch.append(pltpu.VMEM((len(op_axes), *shape), dtype))
+            scratch.append(pltpu.VMEM((len(op_axes), n_max, *shape), dtype))
+            n_sems += sum(sizes[axis] for axis in op_axes)
+        out_shapes.append(jax.ShapeDtypeStruct(tuple(shape), dtype))
+    axes = tuple(dict.fromkeys(axes))
     count = len(ops)
-    n_scratch = len(scratch)
 
     def kernel(*refs):
         ins = refs[:count]
         outs = refs[count : 2 * count]
-        bufs = list(refs[2 * count : 2 * count + n_scratch])
-        send_sem, recv_sem = refs[2 * count + n_scratch :]
+        bufs = refs[2 * count : -2]
+        send_sem, recv_sem = refs[-2:]
         barrier = pltpu.get_barrier_semaphore()
         n_peers = 0
         for axis in axes:
@@ -114,88 +133,151 @@
                 )
                 n_peers += 1
         pl.semaphore_wait(barrier, n_peers)
-
-        def place(ref, index, axis, dim, width, rolled):
+        sends = []
+        used = [0]
+
+        def send(src, dst, land, axis, peer):
+            index = used[0]
+            used[0] += 1
+            make = partial(
+                pltpu.make_async_remote_copy,
+                src_ref=src,
+                send_sem=send_sem.at[index],
+                recv_sem=recv_sem.at[index],
+                device_id={axis: peer},
+                device_id_type=MESH_IDS,
+            )
+            copy = make(dst_ref=dst)
+            copy.start()
+            sends.append(copy)
+            return make(dst_ref=land)
+
+        def peers(axis):
             n = sizes[axis]
-            if rolled:
+            me = lax.axis_index(axis)
+            return [(k, lax.rem(me + k, n), lax.rem(me - k + n, n)) for k in range(1, n)]
+
+        def place(ref, index, axis, dim, width):
+            n = sizes[axis]
+            if axis == "tp":
                 index = lax.rem(index + lax.axis_index("shard") * (n // 2), n)
             start = pl.multiple_of(index * width, width)
             if dim == 0:
                 return ref.at[pl.ds(start, width), :]
             return ref.at[:, pl.ds(start, width)]
 
-        sends = []
-        first = []
-        buf_of = {}
-        for i, (array, axis, kind, dim, rolled) in enumerate(ops):
-            n = sizes[axis]
+        def total_send(i, stage, value):
+            axis = ops[i][1][stage]
+            sent, slots = bufs[slots_of[i] : slots_of[i] + 2]
             me = lax.axis_index(axis)
-            if kind != "gather":
-                buf_of[i] = bufs.pop(0)
-            for k in range(1, n):
-                peer = lax.rem(me + k, n)
-                source = lax.rem(me - k + n, n)
-                if kind == "gather":
-                    width = array.shape[dim]
-                    src = ins[i]
-                    dst = place(outs[i], me, axis, dim, width, rolled)
-                    land = place(outs[i], source, axis, dim, width, rolled)
-                else:
-                    width = array.shape[dim] // n
-                    src = place(ins[i], peer, axis, dim, width, rolled)
-                    dst = buf_of[i].at[k]
-                    land = dst
-                make = partial(
-                    pltpu.make_async_remote_copy,
-                    src_ref=src,
-                    send_sem=send_sem.at[0, i, k],
-                    recv_sem=recv_sem.at[0, i, k],
-                    device_id={axis: peer},
-                    device_id_type=MESH_IDS,
+            sent[stage] = value
+            slots[stage, me] = value
+            return [
+                send(sent.at[stage], slots.at[stage, me], slots.at[stage, source], axis, peer)
+                for k, peer, source in peers(axis)
+            ]
+
+        def total_take(i, stage, pending):
+            slots = bufs[slots_of[i] + 1]
+            for copy in pending:
+                copy.wait_recv()
+            value = slots[stage, 0]
+            for k in range(1, sizes[ops[i][1][stage]]):
+                value = value + slots[stage, k]
+            return value
+
+        pending = {}
+        kinds = {
+            kind: [i for i in range(count) if ops[i][2] == kind]
+            for kind in ("total", "reduce", "scatter", "gather", "grad")
+        }
+        for i in kinds["total"]:
+            pending[i] = total_send(i, 0, ins[i][...])
+        for i in kinds["reduce"] + kinds["scatter"]:
+            array, (axis,), kind, dim = ops[i]
+            width = array.shape[dim] // sizes[axis]
+            buf = bufs[slots_of[i]]
+            pending[i] = [
+                send(place(ins[i], peer, axis, dim, width), buf.at[k], buf.at[k], axis, peer)
+                for k, peer, source in peers(axis)
+            ]
+        for i in kinds["gather"]:
+            array, (axis,), kind, dim = ops[i]
+            width = array.shape[dim]
+            me = lax.axis_index(axis)
+            pending[i] = [
+                send(
+                    ins[i],
+                    place(outs[i], me, axis, dim, width),
+                    place(outs[i], source, axis, dim, width),
+                    axis,
+                    peer,
                 )
-                copy = make(dst_ref=dst)
-                copy.start()
-                sends.append(copy)
-                first.append((i, make(dst_ref=land)))
-        for i, (array, axis, kind, dim, rolled) in enumerate(ops):
-            if kind == "gather":
-                me = lax.axis_index(axis)
-                place(outs[i], me, axis, dim, array.shape[dim], rolled)[...] = ins[i][...]
+                for k, peer, source in peers(axis)
+            ]
+        for i in kinds["grad"]:
+            half = ops[i][0].shape[0] // 2
+            came = bufs[slots_of[i]]
+            other = 1 - lax.axis_index("shard")
+            pending[i] = [send(ins[i].at[pl.ds(half, half), :], came, came, "shard", other)]
+        for i in kinds["gather"]:
+            array, (axis,), kind, dim = ops[i]
+            me = lax.axis_index(axis)
+            place(outs[i], me, axis, dim, array.shape[dim])[...] = ins[i][...]
+        for i in kinds["grad"]:
+            half = ops[i][0].shape[0] // 2
+            came, both, slots = bufs[slots_of[i] : slots_of[i] + 3]
+            pending[i][0].wait_recv()
+            both[...] = (
+                ins[i][pl.ds(0, half), :].astype(jnp.float32) + came[...].astype(jnp.float32)
+            ).astype(both.dtype)
+            width = half // sizes["ctx"]
+            pending[i] = [
+                send(place(both, peer, "ctx", 0, width), slots.at[k], slots.at[k], "ctx", peer)
+                for k, peer, source in peers("ctx")
+            ]
+        value = {}
+        for i in kinds["total"]:
+            value[i] = total_take(i, 0, pending[i])
+            if len(ops[i][1]) > 1:
+                pending[i] = total_send(i, 1, value[i])
         second = []
-        for i, (array, axis, kind, dim, rolled) in enumerate(ops):
-            for j, copy in first:
-                if i == j:
-                    copy.wait_recv()
-            if kind == "gather":
-                continue
-            n = sizes[axis]
+        for i in kinds["reduce"] + kinds["scatter"]:
+            array, (axis,), kind, dim = ops[i]
+            buf = bufs[slots_of[i]]
             me = lax.axis_index(axis)
-            width = array.shape[dim] // n
-            summed = place(ins[i], me, axis, dim, width, rolled)[...].astype(jnp.float32)
-            for k in range(1, n):
-                summed = summed + buf_of[i][k].astype(jnp.float32)
+            width = array.shape[dim] // sizes[axis]
+            for copy in pending[i]:
+                copy.wait_recv()
+            summed = place(ins[i], me, axis, dim, width)[...].astype(jnp.float32)
+            for k in range(1, sizes[axis]):
+                summed = summed + buf[k].astype(jnp.float32)
             if kind == "scatter":
                 outs[i][...] = summed
                 continue
-            mine = place(outs[i], me, axis, dim, width, rolled)
+            mine = place(outs[i], me, axis, dim, width)
             mine[...] = summed.astype(array.dtype)
-            for k in range(1, n):
-                peer = lax.rem(me + k, n)
-                source = lax.rem(me - k + n, n)
-                make = partial(
-                    pltpu.make_async_remote_copy,
-                    src_ref=mine,
-                    send_sem=send_sem.at[1, i, k],
-                    recv_sem=recv_sem.at[1, i, k],
-                    device_id={axis: peer},
-                    device_id_type=MESH_IDS,
-                )
-                copy = make(dst_ref=mine)
-                copy.start()
-                sends.append(copy)
-                second.append(
-                    make(dst_ref=place(outs[i], source, axis, dim, width, rolled))
-                )
+            second += [
+                send(mine, mine, place(outs[i], source, axis, dim, width), axis, peer)
+                for k, peer, source in peers(axis)
+            ]
+        for i in kinds["total"]:
+            for stage in range(1, len(ops[i][1])):
+                value[i] = total_take(i, stage, pending[i])
+                if stage + 1 < len(ops[i][1]):
+                    pending[i] = total_send(i, stage + 1, value[i])
+            outs[i][...] = value[i]
+        for i in kinds["grad"]:
+            both, slots = bufs[slots_of[i] + 1 : slots_of[i] + 3]
+            for copy in pending[i]:
+                copy.wait_recv()
+            width = slots.shape[1]
+            summed = place(both, lax.axis_index("ctx"), "ctx", 0, width)[...].astype(jnp.float32)
+            for k in range(1, sizes["ctx"]):
+                summed = summed + slots[k].astype(jnp.float32)
+            outs[i][...] = summed
+        for i in kinds["gather"]:
+            second += pending[i]
         for copy in second:
             copy.wait_recv()
         for copy in sends:
@@ -208,97 +290,22 @@
         in_specs=[pl.BlockSpec(memory_space=pltpu.VMEM)] * count,
         out_specs=tuple([pl.BlockSpec(memory_space=pltpu.VMEM)] * count),
         scratch_shapes=scratch
-        + [
-            pltpu.SemaphoreType.DMA((2, count, n_max)),
-            pltpu.SemaphoreType.DMA((2, count, n_max)),
-        ],
+        + [pltpu.SemaphoreType.DMA((n_sems,)), pltpu.SemaphoreType.DMA((n_sems,))],
         compiler_params=pltpu.CompilerParams(
-            collective_id=collective_id, has_side_effects=True, vmem_limit_bytes=24 * 1024 * 1024
+            collective_id=collective_id, has_side_effects=True, vmem_limit_bytes=32 * 1024 * 1024
         ),
         cost_estimate=pl.CostEstimate(flops=0, bytes_accessed=8 * total, transcendentals=0),
     )(*[op[0] for op in ops])
 
 
-def total_small(array, sizes):
-    axes = ("tp", "ctx", "shard")
-    n_max = max(sizes[axis] for axis in axes)
-
-    def kernel(in_ref, out_ref, sent, slots, send_sem, recv_sem):
-        barrier = pltpu.get_barrier_semaphore()
-        n_peers = 0
-        for axis in axes:
-            n = sizes[axis]
-            me = lax.axis_index(axis)
-            for k in range(1, n):
-                pl.semaphore_signal(
-                    barrier, inc=1, device_id={axis: lax.rem(me + k, n)}, device_id_type=MESH_IDS
-                )
-                n_peers += 1
-        pl.semaphore_wait(barrier, n_peers)
-        summed = in_ref[...]
-        copies = []
-        for stage, axis in enumerate(axes):
-            n = sizes[axis]
-            me = lax.axis_index(axis)
-            sent[stage] = summed
-            slots[stage, me] = summed
-            here = []
-            for k in range(1, n):
-                make = partial(
-                    pltpu.make_async_remote_copy,
-                    src_ref=sent.at[stage],
-                    send_sem=send_sem.at[stage, k],
-                    recv_sem=recv_sem.at[stage, k],
-                    device_id={axis: lax.rem(me + k, n)},
-                    device_id_type=MESH_IDS,
-                )
-                copy = make(dst_ref=slots.at[stage, me])
-                copy.start()
-                copies.append(copy)
-                here.append(make(dst_ref=slots.at[stage, lax.rem(me - k + n, n)]))
-            for copy in here:
-                copy.wait_recv()
-            summed = slots[stage, 0]
-            for k in range(1, n):
-                summed = summed + slots[stage, k]
-        for copy in copies:
-            copy.wait_send()
-        out_ref[...] = summed
-
-    return pl.pallas_call(
-        kernel,
-        name="sum_gain_gradients",
-        out_shape=jax.ShapeDtypeStruct(array.shape, jnp.float32),
-        in_specs=[pl.BlockSpec(memory_space=pltpu.VMEM)],
-        out_specs=pl.BlockSpec(memory_space=pltpu.VMEM),
-        scratch_shapes=[
-            pltpu.VMEM((len(axes), *array.shape), jnp.float32),
-            pltpu.VMEM((len(axes), n_max, *array.shape), jnp.float32),
-            pltpu.SemaphoreType.DMA((len(axes), n_max)),
-            pltpu.SemaphoreType.DMA((len(axes), n_max)),
-        ],
-        compiler_params=pltpu.CompilerParams(collective_id=6, has_side_effects=True),
-    )(array)
-
-
 def partner(array):
     return lax.ppermute(array, "shard", [(0, 1), (1, 0)])
 
 
-def grad_shard(grad, dim, n_ctx):
-    half = grad.shape[dim] // 2
-    low = grad.astype(jnp.bfloat16)
-    own = lax.slice_in_dim(low, 0, half, axis=dim)
-    theirs = partner(lax.slice_in_dim(low, half, 2 * half, axis=dim))
-    both = (own.astype(jnp.float32) + theirs.astype(jnp.float32)).astype(jnp.bfloat16)
-    width = half // n_ctx
-    me = lax.axis_index("ctx")
-    total = lax.dynamic_slice_in_dim(both, me * width, width, dim).astype(jnp.float32)
-    for k in range(1, n_ctx):
-        piece = lax.dynamic_slice_in_dim(both, (me ^ k) * width, width, dim)
-        came = lax.ppermute(piece, "ctx", [(i, i ^ k) for i in range(n_ctx)])
-        total = total + came.astype(jnp.float32)
-    return total
+GRAD_AXES = ("shard", "ctx")
+ALL_AXES = ("tp", "ctx", "shard")
+TP = ("tp",)
+CTX = ("ctx",)
 
 
 def body(
@@ -341,8 +348,8 @@
         0,
         sizes,
         [
-            (inputs.reshape(local_tokens, width_part), "tp", "gather", 1, True),
-            (packed, "shard", "gather", 0, False),
+            (inputs.reshape(local_tokens, width_part), TP, "gather", 1),
+            (packed, ("shard",), "gather", 0),
         ],
     )
     gains = gains.reshape(2, -1).astype(jnp.float32)
@@ -373,9 +380,9 @@
         1,
         sizes,
         [
-            (key_low, "ctx", "gather", 0, False),
-            (value_low, "ctx", "gather", 0, False),
-            (cotangent.reshape(local_tokens, width_part), "tp", "gather", 1, True),
+            (key_low, CTX, "gather", 0),
+            (value_low, CTX, "gather", 0),
+            (cotangent.reshape(local_tokens, width_part), TP, "gather", 1),
         ],
     )
     kv_local = key_low.shape[1] // HEAD_SIZE
@@ -411,14 +418,14 @@
     attended_low = jnp.concatenate(attended_parts, axis=1).astype(jnp.bfloat16)
     attn_part = jnp.dot(attended_low, w_out, preferred_element_type=jnp.float32)
     mixed = resid_in + exchange(
-        "sum_attention", 2, sizes, [(attn_part.astype(jnp.bfloat16), "tp", "reduce", 1, True)]
+        "sum_attention", 2, sizes, [(attn_part.astype(jnp.bfloat16), TP, "reduce", 1)]
     )[0].astype(jnp.float32)
     normed_mlp_low = rms_norm(mixed, norm_mlp).astype(jnp.bfloat16)
     gate_act = jnp.dot(normed_mlp_low, w_gate, preferred_element_type=jnp.float32)
     up_act = jnp.dot(normed_mlp_low, w_up, preferred_element_type=jnp.float32)
     hidden_low = (jax.nn.silu(gate_act) * up_act).astype(jnp.bfloat16)
     mlp_part = jnp.dot(hidden_low, w_down, preferred_element_type=jnp.float32)
-    d_down = jnp.einsum("tf,td->fd", hidden_low, grad_out, preferred_element_type=jnp.float32)
+    d_down = jnp.einsum("tf,td->df", hidden_low, grad_out, preferred_element_type=jnp.float32)
     d_hidden = jnp.einsum("td,fd->tf", grad_out, w_down, preferred_element_type=jnp.float32)
     sigmoid_gate = jax.nn.sigmoid(gate_act)
     d_gate_low = (
@@ -431,25 +438,22 @@
     d_normed_mlp = d_normed_mlp + jnp.einsum(
         "tf,df->td", d_up_low, w_up, preferred_element_type=jnp.float32
     )
-    mlp_sum, d_normed_mlp = exchange(
+    d_normed_mlp, d_down, d_gate, d_up = exchange(
         "sum_feed_forward",
         3,
         sizes,
         [
-            (mlp_part.astype(jnp.bfloat16), "tp", "scatter", 1, True),
-            (d_normed_mlp.astype(jnp.bfloat16), "tp", "reduce", 1, True),
+            (d_normed_mlp.astype(jnp.bfloat16), TP, "reduce", 1),
+            (d_down.astype(jnp.bfloat16), GRAD_AXES, "grad", 0),
+            (d_gate.astype(jnp.bfloat16), GRAD_AXES, "grad", 0),
+            (d_up.astype(jnp.bfloat16), GRAD_AXES, "grad", 0),
         ],
     )
     d_normed_mlp = d_normed_mlp.astype(jnp.float32)
-    outputs = (
-        (lax.dynamic_slice_in_dim(mixed, feature_start, width_part, 1) + mlp_sum)
-        .astype(jnp.bfloat16)
-        .reshape(1, local_tokens, width_part)
-    )
     d_mix_norm, d_norm_mlp = rms_back(mixed, norm_mlp, d_normed_mlp)
     d_mixed = grad_out.astype(jnp.float32) + d_mix_norm
     d_mixed_low = d_mixed.astype(jnp.bfloat16)
-    d_out = jnp.einsum("th,td->hd", attended_low, d_mixed_low, preferred_element_type=jnp.float32)
+    d_out = jnp.einsum("th,td->dh", attended_low, d_mixed_low, preferred_element_type=jnp.float32)
     d_attended = jnp.einsum(
         "td,hd->th", d_mixed_low, w_out, preferred_element_type=jnp.float32
     ).astype(jnp.bfloat16)
@@ -477,14 +481,20 @@
     d_query_heads = jnp.concatenate(d_query_parts, axis=1)
     d_keys_all = jnp.concatenate(d_key_parts, axis=1)
     d_values_all = jnp.concatenate(d_value_parts, axis=1)
-    d_key_heads, d_value_proj = exchange(
+    d_key_heads, d_value_proj, mlp_sum = exchange(
         "sum_keys_values",
         4,
         sizes,
         [
-            (d_keys_all.astype(jnp.bfloat16), "ctx", "scatter", 0, False),
-            (d_values_all.astype(jnp.bfloat16), "ctx", "scatter", 0, False),
+            (d_keys_all.astype(jnp.bfloat16), CTX, "scatter", 0),
+            (d_values_all.astype(jnp.bfloat16), CTX, "scatter", 0),
+            (mlp_part.astype(jnp.bfloat16), TP, "scatter", 1),
         ],
+    )
+    outputs = (
+        (lax.dynamic_slice_in_dim(mixed, feature_start, width_part, 1) + mlp_sum)
+        .astype(jnp.bfloat16)
+        .reshape(1, local_tokens, width_part)
     )
     d_query_proj, d_gain_query = query_pull(d_query_heads)
     d_key_proj, d_gain_key = key_pull(d_key_heads)
@@ -501,21 +511,40 @@
     d_normed = d_normed + jnp.einsum(
         "th,dh->td", d_value_low, value_weight, preferred_element_type=jnp.float32
     )
-    d_normed = exchange(
-        "sum_input_gradient", 5, sizes, [(d_normed.astype(jnp.bfloat16), "tp", "reduce", 1, True)]
-    )[0].astype(jnp.float32)
-    d_in_norm, d_norm_attn = rms_back(resid_in, norm_attn, d_normed)
-    d_full = d_mixed + d_in_norm
-    d_inputs = (
-        lax.dynamic_slice_in_dim(d_full, feature_start, width_part, 1)
-        .astype(jnp.bfloat16)
-        .reshape(1, local_tokens, width_part)
-    )
-    norms = jnp.stack([d_norm_attn, d_norm_mlp]).reshape(2, 2, width_half) * (1.0 / n_tp)
+    factor = lax.rsqrt(jnp.mean(resid_in * resid_in, axis=-1, keepdims=True) + epsilon)
+    unit_rows = resid_in * factor
+    weighed = d_normed * unit_rows
+    d_norm_attn = jnp.sum(weighed, axis=0)
+    row_part = jnp.sum(weighed * norm_attn, axis=-1).reshape(-1, 128)
+    stat_rows = row_part.shape[0]
+    row_part = jnp.pad(row_part, ((0, -stat_rows % 8), (0, 0)))
+    norms = jnp.stack([d_norm_attn, d_norm_mlp * (1.0 / n_tp)]).reshape(2, 2, width_half)
     norms = jnp.where(shard_index == 0, norms, norms[:, ::-1]).reshape(-1)
     small = jnp.concatenate([norms, d_gain_query, d_gain_key]).reshape(-1, HEAD_SIZE)
     small = jnp.pad(small, ((0, -small.shape[0] % 8), (0, 0)))
-    small = total_small(small, sizes)
+    row_sum, small, d_normed, d_out, d_query, d_key, d_value = exchange(
+        "sum_input_gradient",
+        5,
+        sizes,
+        [
+            (row_part, TP, "total", 0),
+            (small, ALL_AXES, "total", 0),
+            (d_normed.astype(jnp.bfloat16), TP, "scatter", 1),
+            (d_out.astype(jnp.bfloat16), GRAD_AXES, "grad", 0),
+            (d_query.astype(jnp.bfloat16), GRAD_AXES, "grad", 0),
+            (d_key.astype(jnp.bfloat16), GRAD_AXES, "grad", 0),
+            (d_value.astype(jnp.bfloat16), GRAD_AXES, "grad", 0),
+        ],
+    )
+
+    def own_columns(array):
+        return lax.dynamic_slice_in_dim(array, feature_start, width_part, array.ndim - 1)
+
+    row_mean = row_sum[:stat_rows].reshape(local_tokens, 1) / resid_in.shape[1]
+    d_inputs = own_columns(d_mixed) + factor * (
+        d_normed * own_columns(norm_attn) - own_columns(unit_rows) * row_mean
+    )
+    d_inputs = d_inputs.astype(jnp.bfloat16).reshape(1, local_tokens, width_part)
     small = small.reshape(-1)
     place = shard_index * n_ctx + lax.axis_index("ctx")
     full_width = 2 * width_half
@@ -527,13 +556,13 @@
         )
 
     gradients = (
-        grad_shard(d_query, 0, n_ctx),
-        grad_shard(d_key, 0, n_ctx),
-        grad_shard(d_value, 0, n_ctx),
-        grad_shard(d_out, 1, n_ctx),
-        grad_shard(d_gate, 0, n_ctx),
-        grad_shard(d_up, 0, n_ctx),
-        grad_shard(d_down, 1, n_ctx),
+        d_query,
+        d_key,
+        d_value,
+        d_out.T,
+        d_gate,
+        d_up,
+        d_down.T,
         own_part(0, full_width),
         own_part(full_width, full_width),
         own_part(2 * full_width, HEAD_SIZE),

time: 313 us -> 244 us (0.78)
  starting transfers between devices: 28.7 us -> 2.11 us
  waiting for transfers between devices: 26.6 us -> 0.02 us
  Pallas kernels: 150 us -> 131 us
  local copies, waits for them, and re-layouts: 42.1 us -> 54.3 us
  other arithmetic: 30.7 us -> 23.1 us
    ppermute x21 -> x0, waiting for transfers between devices: 26.6 us -> none  [grad_shard(): came = lax.ppermute(piece, 'ctx', [(i, i ^ k) for i in range(n_ctx)])]
    ppermute x21 -> x0, starting transfers between devices: 25.1 us -> none  [grad_shard(): came = lax.ppermute(piece, 'ctx', [(i, i ^ k) for i in range(n_ctx)])]
    pallas_call x1 -> x0, Pallas kernels: 14.8 us -> none  [total_small(): pl.pallas_call(kernel, name='sum_gain_gradients', out_shape=jax.ShapeDtyp...]
    unnamed x167 -> x168, local copies, waits for them, and re-layouts: 19.2 us -> 34 us
    pallas_call x6, Pallas kernels: 136 us -> 131 us  [exchange(): pl.pallas_call(kernel, name=name, out_shape=tuple(out_shapes), in_specs=[...]
    add x7 -> x1, other arithmetic: 5.42 us -> 1.15 us  [body(): resid_in + exchange('sum_attention', 2, sizes, [(attn_part.astype(jnp.bfl...]
  transfers between devices with their start and end apart: 35 -> 7, of which waited for: 15 -> 0; matrix products, arithmetic and copies ran while one was open for 17% -> 18% of each run, Pallas kernels for 19% -> 24%
where the time goes in v2:
time: 244 us; the launch traced here: 243 us
  Pallas kernels  131 us (54%)
  local copies, waits for them, and re-layouts  54.3 us (22%)
  matrix products  30.7 us (13%)
  other arithmetic  23.1 us (9%)
    pallas_call x6, Pallas kernels, exchange(): pl.pallas_call(kernel, name=name, out_shape=tuple(out_shapes), in_specs=[...  131 us
    unnamed x168, local copies, waits for them, and re-layouts  34 us
  transfers between devices with their start and end apart: 7, of which 0 were waited for; matrix products, arithmetic and copies ran while one was open for 18% of the time, Pallas kernels for 24%

profile of v2, /device:TPU:0, one launch (start us, length us, event | category | flops | bytes accessed | tf_op | source)
XLA Modules:
  0.0 243.0 jit_solution(5560909390928645734)
XLA Ops:
  4.1 2.8 %concatenate.64 = bf16[1152]{0:T(1024)(128)(2,1)S(1)} concatenate(bf16[512]{0:T(512)(128)(2,1)} %param.21, bf16[512]{0:T(512)(128)(2,1)} %param.22, bf16[64]{0:T(256)(128)(2,1)} %param.23, bf16[64]{0:T(256)(128)(2,1)} %param.24), dimensions={0} | concatenate | bytes 4608 | tf_op jit(solution)/shard_map/concatenate | solution.py:338
  7.9 14.8 %gather_inputs.1 = (bf16[256,1024]{1,0:T(8,128)(2,1)S(1)}, bf16[32,128]{1,0:T(8,128)(2,1)S(1)}) custom-call(bf16[256,256]{1,0:T(8,128)(2,1)S(1)} %bitcast.165, bf16[16,128]{1,0:T(8,128)(2,1)S(1)} %pad.24.refs_1_), custom_call_target="tpu_custom_call" | custom-call | bytes 540672 | tf_op jit(solution)/shard_map/gather_inputs/pallas_call | solution.py:286
  22.7 1.9 constant_dynamic-update-slice_fusion.1
  24.6 1.9 constant_dynamic-update-slice_fusion.7
  29.8 2.1 constant_dynamic-update-slice_fusion.11
  38.4 18.9 %gather_keys_values.1 = (bf16[1024,256]{1,0:T(8,128)(2,1)S(1)}, bf16[1024,256]{1,0:T(8,128)(2,1)S(1)}, bf16[256,1024]{1,0:T(8,128)(2,1)S(1)}) custom-call(bf16[256,256]{1,0:T(8,128)(2,1)S(1)} %add_convert_fusion.2.refs_0_, bf16[256,256]{1,0:T(8,128)(2,1)S(1)} %convolution_convert_fusion.12.refs_1_, bf16[256,256]{1,0:T(8,128)(2,1)S(1)} %bitcast.164), custom_call_target="tpu_custom_call" | custom-call | bytes 1572864 | tf_op jit(solution)/shard_map/gather_keys_values/pallas_call | solution.py:286
  57.3 1.9 constant_dynamic-update-slice_fusion
  59.2 2.5 %fusion.53 = f32[256,512]{1,0:T(8,128)} fusion(bf16[1024,512]{1,0:T(8,128)(2,1)} %constant_dynamic-update-slice_fusion, f32[1024]{0:T(1024)S(1)} %pad_maximum_fusion.8, f32[256]{0:T(256)S(1)} %add_rsqrt_fusion.1, bf16[256,1024]{1,0:T(8,128)(2,1)S(1)} %get-tuple-element.32), kind=kOutput, calls=%fused_computation.179 | convolution fusion | flops 269484032 | bytes 2102272 | tf_op jit(solution)/shard_map/dot_general | solution.py:369
  65.7 2.5 %fusion.60 = (f32[512]{0:T(512)}, f32[512,1024]{1,0:T(8,128)}) fusion(bf16[512,128]{1,0:T(8,128)(2,1)S(1)} %bitcast.181, bf16[1024,256]{1,0:T(8,128)(2,1)S(1)} %get-tuple-element.34, pred[256,1024]{1,0:T(8,128)(4,1)S(1)} %copy-done.31), kind=kOutput, calls=%fused_computation.186 | convolution fusion | flops 135790080 | bytes 2754560 | tf_op jit(solution)/shard_map/qd,kd->qk/dot_general | solution.py:399
  72.1 2.2 fusion.3
  77.3 2.0 constant_dynamic-update-slice_fusion.6
  79.3 1.7 convolution_convert_fusion.7.refs_0_
  81.0 23.8 %sum_attention.1 = bf16[256,1024]{1,0:T(8,128)(2,1)S(1)} custom-call(bf16[256,1024]{1,0:T(8,128)(2,1)S(1)} %convolution_convert_fusion.7.refs_0_), custom_call_target="tpu_custom_call" | custom-call | bytes 2097152 | tf_op jit(solution)/shard_map/sum_attention/pallas_call | solution.py:286
  116.8 33.2 %sum_feed_forward.1 = (bf16[256,1024]{1,0:T(8,128)(2,1)S(1)}, f32[128,768]{1,0:T(8,128)S(1)}, f32[128,768]{1,0:T(8,128)S(1)}, f32[128,768]{1,0:T(8,128)S(1)}) custom-call(bf16[256,1024]{1,0:T(8,128)(2,1)S(1)} %fusion.5.refs_0_, bf16[1024,768]{1,0:T(8,128)(2,1)S(1)} %convolution_convert_fusion.2.refs_1_, ...), custom_call_target="tpu_custom_call" | custom-call | bytes 20971520 | tf_op jit(solution)/shard_map/sum_feed_forward/pallas_call | solution.py:286
  152.1 1.4 copy-done.24
  162.7 15.8 %sum_keys_values.1 = (f32[256,256]{1,0:T(8,128)S(1)}, f32[256,256]{1,0:T(8,128)S(1)}, f32[256,256]{1,0:T(8,128)S(1)}) custom-call(bf16[1024,256]{1,0:T(8,128)(2,1)S(1)} %pad_maximum_fusion.refs_0_, bf16[1024,256]{1,0:T(8,128)(2,1)S(1)} %pad_maximum_fusion.1.refs_1_, bf16[256,1024]{1,0:T(8,128)(2,1)S(1)} %convolution_convert_fusion.8.refs_2_), custom_call_target="tpu_custom_call" | custom-call | bytes 6291456 | tf_op jit(solution)/shard_map/sum_keys_values/pallas_call | solution.py:286
  190.3 1.7 multiply_reduce_fusion.4
  193.2 1.5 fusion.15
  195.9 3.1 %multiply_reduce_fusion.7 = (f32[1024]{0:T(1024)S(1)}, f32[256]{0:T(256)S(1)}, bf16[256,1024]{1,0:T(8,128)(2,1)S(1)}, f32[256,1024]{1,0:T(8,128)}) fusion(f32[256]{0:T(256)} %copy-done.65, bf16[256,1024]{1,0:T(8,128)(2,1)S(1)} %get-tuple-element.32, f32[1024]{0:T(1024)S(1)} %copy-done.59, f32[256,1024]{1,0:T(8,128)} %fusion.43, f32[256,1024]{1,0:T(8,128)} %fusion.65, ...), kind=kOutput, calls=%fused_computation.79 | convolution fusion | flops 270793472 | bytes 5515264 | tf_op jit(solution)/shard_map/th,dh->td/dot_general | solution.py:507
  202.0 24.4 %sum_input_gradient.1 = (f32[8,128]{1,0:T(8,128)S(1)}, f32[24,128]{1,0:T(8,128)S(1)}, f32[256,256]{1,0:T(8,128)S(1)}, f32[128,512]{1,0:T(8,128)S(1)}, f32[128,51...) custom-call(f32[8,128]{1,0:T(8,128)S(1)} %pad.29.refs_0_, f32[24,128]{1,0:T(8,128)S(1)} %pad.30.refs_1_, ...), custom_call_target="tpu_custom_call" | custom-call | bytes 14712832 | tf_op jit(solution)/shard_map/sum_input_gradient/pallas_call | solution.py:286
  229.8 2.0 copy.127
  234.1 1.8 copy.126
  235.9 1.7 fusion.40
  237.6 1.8 fusion.41
  (304 shorter events, 73.7 us)
Async XLA Ops:
  0.6 25.8 %copy-start.50 = (bf16[512,768]{1,0:T(8,128)(2,1)S(1)}, bf16[512,768]{1,0:T(8,128)(2,1)}, u32[]{:S(2)}) copy-start(bf16[512,768]{1,0:T(8,128)(2,1)} %param.18) | copy-start | bytes 2359300
  0.7 34.2 %collective-permute-start.1 = (bf16[512,256]{1,0:T(8,128)(2,1)}, bf16[512,256]{1,0:T(8,128)(2,1)S(1)}, u32[]{:S(2)}, u32[]{:S(2)}) collective-permute-start(bf16[512,256]{1,0:T(8,128)(2,1)} %param.15), channel_id=1, source_target_pairs={{0,16},{16,0},{1,17},{17,1},{2,18},{18,2},{3,19},{19,3},{4,20},{20... | collective-permute-start | bytes 786440 | tf_op jit(solution)/shard_map/ppermute | solution.py:302
  1.2 35.0 %collective-permute-start.2 = (bf16[512,256]{1,0:T(8,128)(2,1)}, bf16[512,256]{1,0:T(8,128)(2,1)S(1)}, u32[]{:S(2)}, u32[]{:S(2)}) collective-permute-start(bf16[512,256]{1,0:T(8,128)(2,1)} %param.16), channel_id=1, source_target_pairs={{0,16},{16,0},{1,17},{17,1},{2,18},{18,2},{3,19},{19,3},{4,20},{20... | collective-permute-start | bytes 786440 | tf_op jit(solution)/shard_map/ppermute | solution.py:302
  1.3 56.0 %collective-permute-start = (bf16[512,512]{1,0:T(8,128)(2,1)}, bf16[512,512]{1,0:T(8,128)(2,1)}, u32[]{:S(2)}, u32[]{:S(2)}) collective-permute-start(bf16[512,512]{1,0:T(8,128)(2,1)} %param.14), channel_id=1, source_target_pairs={{0,16},{16,0},{1,17},{17,1},{2,18},{18,2},{3,19},{19,3},{4,20},{20... | collective-permute-start | bytes 1572872 | tf_op jit(solution)/shard_map/ppermute | solution.py:302
  1.7 75.6 %collective-permute-start.3 = (bf16[512,512]{1,0:T(8,128)(2,1)}, bf16[512,512]{1,0:T(8,128)(2,1)}, u32[]{:S(2)}, u32[]{:S(2)}) collective-permute-start(bf16[512,512]{1,0:T(8,128)(2,1)} %param.17), channel_id=1, source_target_pairs={{0,16},{16,0},{1,17},{17,1},{2,18},{18,2},{3,19},{19,3},{4,20},{20... | collective-permute-start | bytes 1572872 | tf_op jit(solution)/shard_map/ppermute | solution.py:302
  1.8 104.4 %collective-permute-start.6 = (bf16[512,768]{1,0:T(8,128)(2,1)}, bf16[512,768]{1,0:T(8,128)(2,1)}, u32[]{:S(2)}, u32[]{:S(2)}) collective-permute-start(bf16[512,768]{1,0:T(8,128)(2,1)} %param.18), channel_id=1, source_target_pairs={{0,16},{16,0},{1,17},{17,1},{2,18},{18,2},{3,19},{19,3},{4,20},{20... | collective-permute-start | bytes 2359304 | tf_op jit(solution)/shard_map/ppermute | solution.py:302
  27.4 4.5 %copy-start.51 = (bf16[768,512]{1,0:T(8,128)(2,1)S(1)}, bf16[768,512]{1,0:T(8,128)(2,1)}, u32[]{:S(2)}) copy-start(bf16[768,512]{1,0:T(8,128)(2,1)} %param.20) | copy-start | bytes 2359300
  28.2 5.0 %copy-start.34 = (f32[256,128]{1,0:T(8,128)}, f32[256,128]{1,0:T(8,128)S(1)}, u32[]{:S(2)}) copy-start(f32[256,128]{1,0:T(8,128)S(1)} %pad_maximum_fusion.7) | copy-start | bytes 393220
  28.4 30.8 %copy-start.65 = (f32[256]{0:T(256)}, f32[256]{0:T(256)S(1)}, u32[]{:S(2)}) copy-start(f32[256]{0:T(256)S(1)} %add_rsqrt_fusion.1) | copy-start | bytes 3076
  28.6 6.9 %copy-start.73 = (f32[128]{0:T(128)}, f32[128]{0:T(128)S(1)}, u32[]{:S(2)}) copy-start(f32[128]{0:T(128)S(1)} %mul.469) | copy-start | bytes 1540
  32.9 26.3 %copy-start.58 = (f32[1024]{0:T(1024)}, f32[1024]{0:T(1024)S(1)}, u32[]{:S(2)}) copy-start(f32[1024]{0:T(1024)S(1)} %pad_maximum_fusion.8) | copy-start | bytes 12292
  34.9 75.6 %collective-permute-start.5 = (bf16[512,768]{1,0:T(8,128)(2,1)}, bf16[512,768]{1,0:T(8,128)(2,1)}, u32[]{:S(2)}, u32[]{:S(2)}) collective-permute-start(bf16[512,768]{1,0:T(8,128)(2,1)} %param.19), channel_id=1, source_target_pairs={{0,16},{16,0},{1,17},{17,1},{2,18},{18,2},{3,19},{19,3},{4,20},{20... | collective-permute-start | bytes 2359304 | tf_op jit(solution)/shard_map/ppermute | solution.py:302
  36.2 71.6 %collective-permute-start.4 = (bf16[768,512]{1,0:T(8,128)(2,1)}, bf16[768,512]{1,0:T(8,128)(2,1)}, u32[]{:S(2)}, u32[]{:S(2)}) collective-permute-start(bf16[768,512]{1,0:T(8,128)(2,1)} %param.20), channel_id=1, source_target_pairs={{0,16},{16,0},{1,17},{17,1},{2,18},{18,2},{3,19},{19,3},{4,20},{20... | collective-permute-start | bytes 2359304 | tf_op jit(solution)/shard_map/ppermute | solution.py:302
  72.1 7.2 %copy-start.52 = (bf16[2,256,128]{1,2,0:T(8,128)(2,1)}, bf16[2,256,128]{1,2,0:T(8,128)(2,1)S(1)}, u32[]{:S(2)}) copy-start(bf16[2,256,128]{1,2,0:T(8,128)(2,1)S(1)} %copy.111) | copy-start | bytes 393220
  77.3 28.6 %copy-start.54 = (bf16[2,256,128]{1,2,0:T(8,128)(2,1)}, bf16[2,256,128]{1,2,0:T(8,128)(2,1)S(1)}, u32[]{:S(2)}) copy-start(bf16[2,256,128]{1,2,0:T(8,128)(2,1)S(1)} %copy.113) | copy-start | bytes 393220
  162.5 17.0 %copy-start.42 = (f32[256,128]{0,1:T(8,128)S(1)}, f32[256,128]{0,1:T(8,128)}, u32[]{:S(2)}) copy-start(f32[256,128]{0,1:T(8,128)} %copy-done.41) | copy-start | bytes 393220
  162.6 17.0 %copy-start.40 = (f32[256,128]{0,1:T(8,128)S(1)}, f32[256,128]{0,1:T(8,128)}, u32[]{:S(2)}) copy-start(f32[256,128]{0,1:T(8,128)} %copy-done.39) | copy-start | bytes 393220
  202.0 35.6 %copy-start.67 = (f32[256]{0:T(256)S(1)}, f32[256]{0:T(256)}, u32[]{:S(2)}) copy-start(f32[256]{0:T(256)} %copy-done.65) | copy-start | bytes 3076
  202.0 35.6 %copy-start.74 = (f32[256]{0:T(256)S(1)}, f32[256]{0:T(256)}, u32[]{:S(2)}) copy-start(f32[256]{0:T(256)} %dynamic_slice.30) | copy-start | bytes 3076
  229.7 11.7 %copy-start.3 = (f32[128,768]{1,0:T(8,128)S(1)}, f32[128,768]{1,0:T(8,128)}, u32[]{:S(2)}) copy-start(f32[128,768]{1,0:T(8,128)} %copy-done.2) | copy-start | bytes 1179652
  229.7 7.9 %copy-start.10 = (f32[256,256]{1,0:T(8,128)S(1)}, f32[256,256]{1,0:T(8,128)}, u32[]{:S(2)}) copy-start(f32[256,256]{1,0:T(8,128)} %copy-done.9) | copy-start | bytes 786436
  229.7 9.7 %copy-start.7 = (f32[128,512]{1,0:T(8,128)S(1)}, f32[128,512]{1,0:T(8,128)}, u32[]{:S(2)}) copy-start(f32[128,512]{1,0:T(8,128)} %copy-done.6) | copy-start | bytes 786436
  229.7 10.4 %copy-start.16 = (f32[128,256]{1,0:T(8,128)S(1)}, f32[128,256]{1,0:T(8,128)}, u32[]{:S(2)}) copy-start(f32[128,256]{1,0:T(8,128)} %copy-done.15) | copy-start | bytes 393220
  229.7 11.1 %copy-start.14 = (f32[128,256]{1,0:T(8,128)S(1)}, f32[128,256]{1,0:T(8,128)}, u32[]{:S(2)}) copy-start(f32[128,256]{1,0:T(8,128)} %copy-done.13) | copy-start | bytes 393220
  (58 other events, 108.1 us)

commit v3 on v2

--- a/solution.py
+++ b/solution.py
@@ -92,6 +92,9 @@
         if kind == "gather":
             shape[dim] *= n
             n_sems += n
+        elif kind == "pair":
+            shape[dim] *= 2
+            n_sems += 1
         elif kind == "scatter":
             shape[dim] //= n
             scratch.append(pltpu.VMEM((n, *shape), dtype))
@@ -189,7 +192,7 @@
         pending = {}
         kinds = {
             kind: [i for i in range(count) if ops[i][2] == kind]
-            for kind in ("total", "reduce", "scatter", "gather", "grad")
+            for kind in ("total", "reduce", "scatter", "gather", "pair", "grad")
         }
         for i in kinds["total"]:
             pending[i] = total_send(i, 0, ins[i][...])
@@ -215,6 +218,12 @@
                 )
                 for k, peer, source in peers(axis)
             ]
+        for i in kinds["pair"]:
+            array, axis, kind, dim = ops[i]
+            width = array.shape[dim]
+            second_half = pl.ds(width, width)
+            dst = outs[i].at[second_half, :] if dim == 0 else outs[i].at[:, second_half]
+            pending[i] = [send(ins[i], dst, dst, "shard", 1 - lax.axis_index("shard"))]
         for i in kinds["grad"]:
             half = ops[i][0].shape[0] // 2
             came = bufs[slots_of[i]]
@@ -224,6 +233,13 @@
             array, (axis,), kind, dim = ops[i]
             me = lax.axis_index(axis)
             place(outs[i], me, axis, dim, array.shape[dim])[...] = ins[i][...]
+        for i in kinds["pair"]:
+            array, axis, kind, dim = ops[i]
+            first_half = pl.ds(0, array.shape[dim])
+            if dim == 0:
+                outs[i][first_half, :] = ins[i][...]
+            else:
+                outs[i][:, first_half] = ins[i][...]
         for i in kinds["grad"]:
             half = ops[i][0].shape[0] // 2
             came, both, slots = bufs[slots_of[i] : slots_of[i] + 3]
@@ -276,7 +292,7 @@
             for k in range(1, sizes["ctx"]):
                 summed = summed + slots[k].astype(jnp.float32)
             outs[i][...] = summed
-        for i in kinds["gather"]:
+        for i in kinds["gather"] + kinds["pair"]:
             second += pending[i]
         for copy in second:
             copy.wait_recv()
@@ -298,10 +314,7 @@
     )(*[op[0] for op in ops])
 
 
-def partner(array):
-    return lax.ppermute(array, "shard", [(0, 1), (1, 0)])
-
-
+SHARD = ("shard",)
 GRAD_AXES = ("shard", "ctx")
 ALL_AXES = ("tp", "ctx", "shard")
 TP = ("tp",)
@@ -327,13 +340,6 @@
     n_ctx = sizes["ctx"]
     n_tp = sizes["tp"]
     shard_index = lax.axis_index("shard")
-    w_query = jnp.concatenate([w_query, partner(w_query)], axis=0)
-    key_weight = jnp.concatenate([key_weight, partner(key_weight)], axis=0)
-    value_weight = jnp.concatenate([value_weight, partner(value_weight)], axis=0)
-    w_out = jnp.concatenate([w_out, partner(w_out)], axis=1)
-    w_gate = jnp.concatenate([w_gate, partner(w_gate)], axis=0)
-    w_up = jnp.concatenate([w_up, partner(w_up)], axis=0)
-    w_down = jnp.concatenate([w_down, partner(w_down)], axis=1)
     width_half = norm_attn.shape[0]
     packed = jnp.concatenate([norm_attn, norm_mlp, gain_query, gain_key]).reshape(-1, HEAD_SIZE)
     pack_rows = packed.shape[0]
@@ -343,13 +349,16 @@
     offset = lax.axis_index("ctx") * local_tokens
     query_pos = offset + jnp.arange(local_tokens, dtype=jnp.int32)
     positions = query_pos.astype(jnp.float32)
-    full_in, gains = exchange(
+    full_in, gains, w_query, key_weight, value_weight = exchange(
         "gather_inputs",
         0,
         sizes,
         [
             (inputs.reshape(local_tokens, width_part), TP, "gather", 1),
-            (packed, ("shard",), "gather", 0),
+            (packed, SHARD, "gather", 0),
+            (w_query, SHARD, "pair", 0),
+            (key_weight, SHARD, "pair", 0),
+            (value_weight, SHARD, "pair", 0),
         ],
     )
     gains = gains.reshape(2, -1).astype(jnp.float32)
@@ -375,7 +384,7 @@
     query_low = query_heads.astype(jnp.bfloat16)
     key_low = key_heads.astype(jnp.bfloat16)
     value_low = value_proj.astype(jnp.bfloat16)
-    key_all, value_all, grad_out = exchange(
+    key_all, value_all, grad_out, w_out, w_gate, w_up, w_down = exchange(
         "gather_keys_values",
         1,
         sizes,
@@ -383,6 +392,10 @@
             (key_low, CTX, "gather", 0),
             (value_low, CTX, "gather", 0),
             (cotangent.reshape(local_tokens, width_part), TP, "gather", 1),
+            (w_out, SHARD, "pair", 1),
+            (w_gate, SHARD, "pair", 0),
+            (w_up, SHARD, "pair", 0),
+            (w_down, SHARD, "pair", 1),
         ],
     )
     kv_local = key_low.shape[1] // HEAD_SIZE

time: 244 us -> 215 us (0.88)
  local copies, waits for them, and re-layouts: 54.3 us -> 33.6 us
  matrix products: 30.7 us -> 22.9 us
    unnamed x168 -> x199, local copies, waits for them, and re-layouts: 34 us -> 18.3 us
    concatenate x7 -> x0, local copies, waits for them, and re-layouts: 7.49 us -> none  [the longest x1 1.98 us: body(): w_out = jnp.concatenate([w_out, partner(w_out)], axis=1)]
    dot_general x1, matrix products: 3.09 us -> 0.47 us  [body(): jnp.einsum('th,dh->td', d_query_low, w_query, preferred_element_type=jnp....]
  transfers between devices with their start and end apart: 7 -> 0, of which waited for: 0 -> 0; matrix products, arithmetic and copies ran while one was open for 18% -> 0% of each run, Pallas kernels for 24% -> 0%
where the time goes in v3:
time: 215 us; the launch traced here: 214 us
  Pallas kernels  131 us (61%)
  local copies, waits for them, and re-layouts  33.6 us (16%)
  other arithmetic  24.9 us (12%)
  matrix products  22.9 us (11%)
  between operations  2.29 us (1%)
    pallas_call x6, Pallas kernels, exchange(): pl.pallas_call(kernel, name=name, out_shape=tuple(out_shapes), in_specs=[...  131 us
    unnamed x199, local copies, waits for them, and re-layouts  18.3 us

profile of v3, /device:TPU:0, one launch (start us, length us, event | category | flops | bytes accessed | tf_op | source)
XLA Modules:
  0.0 214.5 jit_solution(13718955328022793090)
XLA Ops:
  0.7 2.9 %concatenate.43 = bf16[1152]{0:T(1024)(128)(2,1)S(1)} concatenate(bf16[512]{0:T(512)(128)(2,1)} %param.21, bf16[512]{0:T(512)(128)(2,1)} %param.22, bf16[64]{0:T(256)(128)(2,1)} %param.23, bf16[64]{0:T(256)(128)(2,1)} %param.24), dimensions={0} | concatenate | bytes 4608 | tf_op jit(solution)/shard_map/concatenate | solution.py:344
  8.9 15.2 %gather_inputs.1 = (bf16[256,1024]{1,0:T(8,128)(2,1)S(1)}, bf16[32,128]{1,0:T(8,128)(2,1)S(1)}, bf16[1024,512]{1,0:T(8,128)(2,1)S(1)}, bf16[1024,256]{1,0:T(8,128)(2,1)S(1)}, bf16[1024,256]{1,0:T(8,128)(2,1)S(1)}) custom-call(bf16[256,256]{1,0:T(8,128)(2,1)S(1)} %bitcast.162, bf16[16,128]{1,0:T(8,128)(2,1)S(1)} %pad.24.refs_1_, ...), custom_call_target="tpu_custom_call" | custom-call | bytes 4734976 | tf_op jit(solution)/shard_map/gather_inputs/pallas_call | solution.py:302
  34.4 17.3 %gather_keys_values.1 = (bf16[1024,256]{1,0:T(8,128)(2,1)S(1)}, bf16[1024,256]{1,0:T(8,128)(2,1)S(1)}, bf16[256,1024]{1,0:T(8,128)(2,1)S(1)}, bf16[512,1024]{1,0...) custom-call(bf16[256,256]{1,0:T(8,128)(2,1)S(1)} %add_convert_fusion, ...), custom_call_target="tpu_custom_call" | custom-call | bytes 13107200 | tf_op jit(solution)/shard_map/gather_keys_values/pallas_call | solution.py:302
  51.7 1.9 fusion.61
  58.3 2.0 fusion.2
  61.9 1.7 convolution_convert_fusion.7.refs_0_
  63.7 23.3 %sum_attention.1 = bf16[256,1024]{1,0:T(8,128)(2,1)S(1)} custom-call(bf16[256,1024]{1,0:T(8,128)(2,1)S(1)} %convolution_convert_fusion.7.refs_0_), custom_call_target="tpu_custom_call" | custom-call | bytes 2097152 | tf_op jit(solution)/shard_map/sum_attention/pallas_call | solution.py:302
  87.0 1.2 convert_add_fusion
  92.1 1.4 convolution_convert_fusion.8.refs_2_
  95.4 33.8 %sum_feed_forward.1 = (bf16[256,1024]{1,0:T(8,128)(2,1)S(1)}, f32[128,768]{1,0:T(8,128)S(1)}, f32[128,768]{1,0:T(8,128)S(1)}, f32[128,768]{1,0:T(8,128)S(1)}) custom-call(bf16[256,1024]{1,0:T(8,128)(2,1)S(1)} %fusion.4.refs_0_, bf16[1024,768]{1,0:T(8,128)(2,1)S(1)} %convolution_convert_fusion.2.refs_1_, ...), custom_call_target="tpu_custom_call" | custom-call | bytes 20971520 | tf_op jit(solution)/shard_map/sum_feed_forward/pallas_call | solution.py:302
  130.7 1.1 fusion.12
  132.4 1.3 mul.537
  134.4 1.1 fusion.11
  136.0 1.4 copy-done.39
  138.5 1.0 copy-done.37
  143.1 1.0 copy-done.33
  146.2 16.5 %sum_keys_values.1 = (f32[256,256]{1,0:T(8,128)S(1)}, f32[256,256]{1,0:T(8,128)S(1)}, f32[256,256]{1,0:T(8,128)S(1)}) custom-call(bf16[1024,256]{1,0:T(8,128)(2,1)S(1)} %pad_maximum_fusion.refs_0_, bf16[1024,256]{1,0:T(8,128)(2,1)S(1)} %pad_maximum_fusion.1.refs_1_, bf16[256,1024]{1,0:T(8,128)(2,1)S(1)} %copy-done.4), custom_call_target="tpu_custom_call" | custom-call | bytes 6291456 | tf_op jit(solution)/shard_map/sum_keys_values/pallas_call | solution.py:302
  162.8 1.8 fusion.40
  169.6 2.5 %multiply_reduce_fusion.4 = (f32[128]{0:T(128)}, f32[256,4]{1,0:T(8,128)}, f32[256,4,128]{2,1,0:T(4,128)}) fusion(f32[256,4,128]{2,1,0:T(4,128)S(1)} %copy-done.41, f32[256,4]{1,0:T(8,128)S(1)} %copy-done.46, f32[128]{0:T(128)S(1)} %copy-done.88, f32[256,4,64]{2,1,0:T(4,128)S(1)} %get-tuple-element.148, f32[256,4,64]{2,1,0:T(4,128)S(1)} %get-tuple-element.147, ...), kind=kLoop, calls=%fused_computation.71 | loop fusion | flops 1309568 | bytes 2237440 | tf_op jit(solution)/shard_map/transpose(jvp())/reduce_sum | solution.py:20
  173.9 1.8 fusion.14
  177.0 1.5 multiply_reduce_fusion.7
  179.4 1.7 convolution_convert_fusion.4.refs_3_
  181.1 24.8 %sum_input_gradient.1 = (f32[8,128]{1,0:T(8,128)S(1)}, f32[24,128]{1,0:T(8,128)S(1)}, f32[256,256]{1,0:T(8,128)S(1)}, f32[128,512]{1,0:T(8,128)S(1)}, f32[128,51...) custom-call(f32[8,128]{1,0:T(8,128)S(1)} %pad.29.refs_0_, f32[24,128]{1,0:T(8,128)S(1)} %pad.30.refs_1_, ...), custom_call_target="tpu_custom_call" | custom-call | bytes 14712832 | tf_op jit(solution)/shard_map/sum_input_gradient/pallas_call | solution.py:302
  205.9 1.9 fusion.41
  (314 shorter events, 52.2 us)
Async XLA Ops:
  0.6 7.3 %copy-start.28 = (bf16[512,256]{1,0:T(8,128)(2,1)S(1)}, bf16[512,256]{1,0:T(8,128)(2,1)}, u32[]{:S(2)}) copy-start(bf16[512,256]{1,0:T(8,128)(2,1)} %refs_3_.2) | copy-start | bytes 786436
  0.7 7.3 %copy-start.19 = (bf16[512,512]{1,0:T(8,128)(2,1)S(1)}, bf16[512,512]{1,0:T(8,128)(2,1)}, u32[]{:S(2)}) copy-start(bf16[512,512]{1,0:T(8,128)(2,1)} %refs_2_.1) | copy-start | bytes 1572868
  0.7 7.3 %copy-start.30 = (bf16[1,256,256]{2,1,0:T(8,128)(2,1)S(1)}, bf16[1,256,256]{2,1,0:T(8,128)(2,1)}, u32[]{:S(2)}) copy-start(bf16[1,256,256]{2,1,0:T(8,128)(2,1)} %param.13) | copy-start | bytes 393220
  24.1 4.1 %copy-start.17 = (bf16[1024,256]{1,0:T(8,128)(2,1)}, bf16[1024,256]{1,0:T(8,128)(2,1)S(1)}, u32[]{:S(2)}) copy-start(bf16[1024,256]{1,0:T(8,128)(2,1)S(1)} %get-tuple-element.43) | copy-start | bytes 1572868
  24.1 4.1 %copy-start.20 = (bf16[1024,256]{1,0:T(8,128)(2,1)}, bf16[1024,256]{1,0:T(8,128)(2,1)S(1)}, u32[]{:S(2)}) copy-start(bf16[1024,256]{1,0:T(8,128)(2,1)S(1)} %get-tuple-element.42) | copy-start | bytes 1572868
  24.1 5.6 %copy-start.9 = (bf16[1024,512]{1,0:T(8,128)(2,1)}, bf16[1024,512]{1,0:T(8,128)(2,1)S(1)}, u32[]{:S(2)}) copy-start(bf16[1024,512]{1,0:T(8,128)(2,1)S(1)} %get-tuple-element.41) | copy-start | bytes 3145732
  24.3 5.4 %copy-start.80 = (f32[256]{0:T(256)}, f32[256]{0:T(256)S(1)}, u32[]{:S(2)}) copy-start(f32[256]{0:T(256)S(1)} %add_rsqrt_fusion.1) | copy-start | bytes 3076
  26.0 3.8 %copy-start.72 = (f32[1024]{0:T(1024)}, f32[1024]{0:T(1024)S(1)}, u32[]{:S(2)}) copy-start(f32[1024]{0:T(1024)S(1)} %pad_maximum_fusion.8) | copy-start | bytes 12292
  32.9 22.0 %copy-start.57 = (bf16[32,2,8,128]{3,2,0,1:T(8,128)(2,1)}, bf16[32,2,8,128]{3,2,0,1:T(8,128)(2,1)S(1)}, u32[]{:S(2)}) copy-start(bf16[32,2,8,128]{3,2,0,1:T(8,128)(2,1)S(1)} %copy.167) | copy-start | bytes 393220
  32.9 20.7 %copy-start.59 = (bf16[32,2,8,128]{3,2,0,1:T(8,128)(2,1)}, bf16[32,2,8,128]{3,2,0,1:T(8,128)(2,1)S(1)}, u32[]{:S(2)}) copy-start(bf16[32,2,8,128]{3,2,0,1:T(8,128)(2,1)S(1)} %copy.166) | copy-start | bytes 393220
  51.7 8.7 %copy-start.2 = (bf16[1024,256]{1,0:T(8,128)(2,1)}, bf16[1024,256]{1,0:T(8,128)(2,1)S(1)}, u32[]{:S(2)}) copy-start(bf16[1024,256]{1,0:T(8,128)(2,1)S(1)} %get-tuple-element.45) | copy-start | bytes 1572868
  54.3 4.0 %copy-start.70 = (f32[512]{0:T(512)}, f32[512]{0:T(512)S(1)}, u32[]{:S(2)}) copy-start(f32[512]{0:T(512)S(1)} %get-tuple-element.175) | copy-start | bytes 6148
  61.9 26.3 %copy-start.66 = (bf16[2,256,128]{1,2,0:T(8,128)(2,1)}, bf16[2,256,128]{1,2,0:T(8,128)(2,1)S(1)}, u32[]{:S(2)}) copy-start(bf16[2,256,128]{1,2,0:T(8,128)(2,1)S(1)} %copy.113) | copy-start | bytes 393220
  88.2 42.5 %copy-start.79 = (f32[256]{0:T(256)}, f32[256]{0:T(256)S(1)}, u32[]{:S(2)}) copy-start(f32[256]{0:T(256)S(1)} %add_rsqrt_fusion) | copy-start | bytes 3076
  130.7 4.7 %copy-start.12 = (bf16[512,1024]{1,0:T(8,128)(2,1)S(1)}, bf16[512,1024]{1,0:T(8,128)(2,1)}, u32[]{:S(2)}) copy-start(bf16[512,1024]{1,0:T(8,128)(2,1)} %copy-done.11) | copy-start | bytes 3145732
  146.2 19.5 %copy-start.44 = (f32[256,256]{0,1:T(8,128)S(1)}, f32[256,256]{0,1:T(8,128)}, u32[]{:S(2)}) copy-start(f32[256,256]{0,1:T(8,128)} %copy-done.43) | copy-start | bytes 786436
  146.2 19.5 %copy-start.55 = (f32[256,128]{0,1:T(8,128)S(1)}, f32[256,128]{0,1:T(8,128)}, u32[]{:S(2)}) copy-start(f32[256,128]{0,1:T(8,128)} %copy-done.54) | copy-start | bytes 393220
  162.7 5.7 %copy-start.26 = (f32[256,256]{1,0:T(8,128)}, f32[256,256]{1,0:T(8,128)S(1)}, u32[]{:S(2)}) copy-start(f32[256,256]{1,0:T(8,128)S(1)} %get-tuple-element.54) | copy-start | bytes 786436
  162.8 3.9 %copy-start.84 = (f32[256,2]{0,1:T(2,128)S(1)}, f32[256,2]{0,1:T(2,128)}, u32[]{:S(2)}) copy-start(f32[256,2]{0,1:T(2,128)} %copy-done.83) | copy-start | bytes 6148
  162.8 4.0 %copy-start.53 = (f32[256,128]{1,0:T(8,128)S(1)}, f32[256,128]{1,0:T(8,128)}, u32[]{:S(2)}) copy-start(f32[256,128]{1,0:T(8,128)} %copy-done.51) | copy-start | bytes 393220
  169.6 6.2 %copy-start.10 = (bf16[1024,512]{1,0:T(8,128)(2,1)S(1)}, bf16[1024,512]{1,0:T(8,128)(2,1)}, u32[]{:S(2)}) copy-start(bf16[1024,512]{1,0:T(8,128)(2,1)} %copy-done.9) | copy-start | bytes 3145732
  172.0 4.4 %copy-start.21 = (bf16[1024,256]{1,0:T(8,128)(2,1)S(1)}, bf16[1024,256]{1,0:T(8,128)(2,1)}, u32[]{:S(2)}) copy-start(bf16[1024,256]{1,0:T(8,128)(2,1)} %copy-done.20) | copy-start | bytes 1572868
  181.1 24.8 %copy-start.91 = (f32[256]{0:T(256)S(1)}, f32[256]{0:T(256)}, u32[]{:S(2)}) copy-start(f32[256]{0:T(256)} %dynamic_slice.30) | copy-start | bytes 3076
  205.9 7.1 %copy-start.23 = (f32[128,768]{1,0:T(8,128)S(1)}, f32[128,768]{1,0:T(8,128)}, u32[]{:S(2)}) copy-start(f32[128,768]{1,0:T(8,128)} %copy-done.22) | copy-start | bytes 1179652
  (70 other events, 118.8 us)

commit v4 on v3

--- a/solution.py
+++ b/solution.py
@@ -494,20 +494,14 @@
     d_query_heads = jnp.concatenate(d_query_parts, axis=1)
     d_keys_all = jnp.concatenate(d_key_parts, axis=1)
     d_values_all = jnp.concatenate(d_value_parts, axis=1)
-    d_key_heads, d_value_proj, mlp_sum = exchange(
+    d_key_heads, d_value_proj = exchange(
         "sum_keys_values",
         4,
         sizes,
         [
             (d_keys_all.astype(jnp.bfloat16), CTX, "scatter", 0),
             (d_values_all.astype(jnp.bfloat16), CTX, "scatter", 0),
-            (mlp_part.astype(jnp.bfloat16), TP, "scatter", 1),
         ],
-    )
-    outputs = (
-        (lax.dynamic_slice_in_dim(mixed, feature_start, width_part, 1) + mlp_sum)
-        .astype(jnp.bfloat16)
-        .reshape(1, local_tokens, width_part)
     )
     d_query_proj, d_gain_query = query_pull(d_query_heads)
     d_key_proj, d_gain_key = key_pull(d_key_heads)
@@ -535,7 +529,7 @@
     norms = jnp.where(shard_index == 0, norms, norms[:, ::-1]).reshape(-1)
     small = jnp.concatenate([norms, d_gain_query, d_gain_key]).reshape(-1, HEAD_SIZE)
     small = jnp.pad(small, ((0, -small.shape[0] % 8), (0, 0)))
-    row_sum, small, d_normed, d_out, d_query, d_key, d_value = exchange(
+    row_sum, small, d_normed, mlp_sum, d_out, d_query, d_key, d_value = exchange(
         "sum_input_gradient",
         5,
         sizes,
@@ -543,11 +537,18 @@
             (row_part, TP, "total", 0),
             (small, ALL_AXES, "total", 0),
             (d_normed.astype(jnp.bfloat16), TP, "scatter", 1),
+            (mlp_part.astype(jnp.bfloat16), TP, "scatter", 1),
             (d_out.astype(jnp.bfloat16), GRAD_AXES, "grad", 0),
             (d_query.astype(jnp.bfloat16), GRAD_AXES, "grad", 0),
             (d_key.astype(jnp.bfloat16), GRAD_AXES, "grad", 0),
             (d_value.astype(jnp.bfloat16), GRAD_AXES, "grad", 0),
         ],
+    )
+
+    outputs = (
+        (lax.dynamic_slice_in_dim(mixed, feature_start, width_part, 1) + mlp_sum)
+        .astype(jnp.bfloat16)
+        .reshape(1, local_tokens, width_part)
     )
 
     def own_columns(array):

time: 215 us -> 217 us (level)
    pallas_call x6, Pallas kernels: 131 us -> 133 us  [exchange(): pl.pallas_call(kernel, name=name, out_shape=tuple(out_shapes), in_specs=[...]
    unnamed x199 -> x203, local copies, waits for them, and re-layouts: 18.3 us -> 19.1 us
where the time goes in v4:
time: 217 us; the launch traced here: 216 us
  Pallas kernels  133 us (61%)
  local copies, waits for them, and re-layouts  34.4 us (16%)
  other arithmetic  23.6 us (11%)
  matrix products  22.9 us (11%)
  between operations  2.33 us (1%)
    pallas_call x6, Pallas kernels, exchange(): pl.pallas_call(kernel, name=name, out_shape=tuple(out_shapes), in_specs=[...  133 us
    unnamed x203, local copies, waits for them, and re-layouts  19.1 us

profile of v4, /device:TPU:0, one launch (start us, length us, event | category | flops | bytes accessed | tf_op | source)
XLA Modules:
  0.0 216.2 jit_solution(15322831542066631166)
XLA Ops:
  0.7 2.9 %concatenate.43 = bf16[1152]{0:T(1024)(128)(2,1)S(1)} concatenate(bf16[512]{0:T(512)(128)(2,1)} %param.21, bf16[512]{0:T(512)(128)(2,1)} %param.22, bf16[64]{0:T(256)(128)(2,1)} %param.23, bf16[64]{0:T(256)(128)(2,1)} %param.24), dimensions={0} | concatenate | bytes 4608 | tf_op jit(solution)/shard_map/concatenate | solution.py:344
  8.9 15.2 %gather_inputs.1 = (bf16[256,1024]{1,0:T(8,128)(2,1)S(1)}, bf16[32,128]{1,0:T(8,128)(2,1)S(1)}, bf16[1024,512]{1,0:T(8,128)(2,1)S(1)}, bf16[1024,256]{1,0:T(8,128)(2,1)S(1)}, bf16[1024,256]{1,0:T(8,128)(2,1)S(1)}) custom-call(bf16[256,256]{1,0:T(8,128)(2,1)S(1)} %bitcast.162, bf16[16,128]{1,0:T(8,128)(2,1)S(1)} %pad.24.refs_1_, ...), custom_call_target="tpu_custom_call" | custom-call | bytes 4734976 | tf_op jit(solution)/shard_map/gather_inputs/pallas_call | solution.py:302
  34.4 17.3 %gather_keys_values.1 = (bf16[1024,256]{1,0:T(8,128)(2,1)S(1)}, bf16[1024,256]{1,0:T(8,128)(2,1)S(1)}, bf16[256,1024]{1,0:T(8,128)(2,1)S(1)}, bf16[512,1024]{1,0...) custom-call(bf16[256,256]{1,0:T(8,128)(2,1)S(1)} %add_convert_fusion, ...), custom_call_target="tpu_custom_call" | custom-call | bytes 13107200 | tf_op jit(solution)/shard_map/gather_keys_values/pallas_call | solution.py:302
  51.7 1.9 fusion.61
  58.3 2.0 fusion.2
  61.9 1.7 convolution_convert_fusion.7.refs_0_
  63.7 23.3 %sum_attention.1 = bf16[256,1024]{1,0:T(8,128)(2,1)S(1)} custom-call(bf16[256,1024]{1,0:T(8,128)(2,1)S(1)} %convolution_convert_fusion.7.refs_0_), custom_call_target="tpu_custom_call" | custom-call | bytes 2097152 | tf_op jit(solution)/shard_map/sum_attention/pallas_call | solution.py:302
  87.0 1.2 convert_add_fusion
  92.1 1.4 convolution_convert_fusion.8.refs_3_
  95.4 33.9 %sum_feed_forward.1 = (bf16[256,1024]{1,0:T(8,128)(2,1)S(1)}, f32[128,768]{1,0:T(8,128)S(1)}, f32[128,768]{1,0:T(8,128)S(1)}, f32[128,768]{1,0:T(8,128)S(1)}) custom-call(bf16[256,1024]{1,0:T(8,128)(2,1)S(1)} %fusion.4.refs_0_, bf16[1024,768]{1,0:T(8,128)(2,1)S(1)} %convolution_convert_fusion.2.refs_1_, ...), custom_call_target="tpu_custom_call" | custom-call | bytes 20971520 | tf_op jit(solution)/shard_map/sum_feed_forward/pallas_call | solution.py:302
  130.8 1.1 fusion.12
  132.5 1.3 mul.536
  136.0 1.4 copy-done.40
  138.5 1.0 copy-done.38
  143.1 1.0 copy-done.34
  146.0 16.3 %sum_keys_values.1 = (f32[256,256]{1,0:T(8,128)S(1)}, f32[256,256]{1,0:T(8,128)S(1)}) custom-call(bf16[1024,256]{1,0:T(8,128)(2,1)S(1)} %pad_maximum_fusion.1.refs_0_, bf16[1024,256]{1,0:T(8,128)(2,1)S(1)} %pad_maximum_fusion.2.refs_1_), custom_call_target="tpu_custom_call" | custom-call | bytes 4194304 | tf_op jit(solution)/shard_map/sum_keys_values/pallas_call | solution.py:302
  166.5 2.4 %multiply_reduce_fusion.4 = (f32[128]{0:T(128)}, f32[256,4]{1,0:T(8,128)}, f32[256,4,128]{2,1,0:T(4,128)}) fusion(f32[256,4,128]{2,1,0:T(4,128)S(1)} %copy-done.42, f32[256,4]{1,0:T(8,128)S(1)} %copy-done.47, f32[128]{0:T(128)S(1)} %copy-done.90, f32[256,4,64]{2,1,0:T(4,128)S(1)} %get-tuple-element.148, f32[256,4,64]{2,1,0:T(4,128)S(1)} %get-tuple-element.147, ...), kind=kLoop, calls=%fused_computation.71 | loop fusion | flops 1309568 | bytes 2237440 | tf_op jit(solution)/shard_map/transpose(jvp())/reduce_sum | solution.py:20
  170.8 1.8 fusion.14
  173.9 1.4 multiply_reduce_fusion.7
  176.3 1.7 convolution_convert_fusion.4.refs_4_
  178.0 27.0 %sum_input_gradient.1 = (f32[8,128]{1,0:T(8,128)S(1)}, f32[24,128]{1,0:T(8,128)S(1)}, f32[256,256]{1,0:T(8,128)S(1)}, f32[256,256]{1,0:T(8,128)S(1)}, f32[128,51...) custom-call(f32[8,128]{1,0:T(8,128)S(1)} %pad.29.refs_0_, ...), custom_call_target="tpu_custom_call" | custom-call | bytes 16809984 | tf_op jit(solution)/shard_map/sum_input_gradient/pallas_call | solution.py:302
  205.0 1.7 fusion.40
  206.7 1.8 fusion.41
  212.5 1.6 copy.175
  (318 shorter events, 51.5 us)
Async XLA Ops:
  0.6 7.3 %copy-start.28 = (bf16[512,256]{1,0:T(8,128)(2,1)S(1)}, bf16[512,256]{1,0:T(8,128)(2,1)}, u32[]{:S(2)}) copy-start(bf16[512,256]{1,0:T(8,128)(2,1)} %refs_3_.2) | copy-start | bytes 786436
  0.7 7.3 %copy-start.19 = (bf16[512,512]{1,0:T(8,128)(2,1)S(1)}, bf16[512,512]{1,0:T(8,128)(2,1)}, u32[]{:S(2)}) copy-start(bf16[512,512]{1,0:T(8,128)(2,1)} %refs_2_.1) | copy-start | bytes 1572868
  0.7 7.3 %copy-start.30 = (bf16[1,256,256]{2,1,0:T(8,128)(2,1)S(1)}, bf16[1,256,256]{2,1,0:T(8,128)(2,1)}, u32[]{:S(2)}) copy-start(bf16[1,256,256]{2,1,0:T(8,128)(2,1)} %param.13) | copy-start | bytes 393220
  24.1 4.1 %copy-start.17 = (bf16[1024,256]{1,0:T(8,128)(2,1)}, bf16[1024,256]{1,0:T(8,128)(2,1)S(1)}, u32[]{:S(2)}) copy-start(bf16[1024,256]{1,0:T(8,128)(2,1)S(1)} %get-tuple-element.43) | copy-start | bytes 1572868
  24.1 4.1 %copy-start.20 = (bf16[1024,256]{1,0:T(8,128)(2,1)}, bf16[1024,256]{1,0:T(8,128)(2,1)S(1)}, u32[]{:S(2)}) copy-start(bf16[1024,256]{1,0:T(8,128)(2,1)S(1)} %get-tuple-element.42) | copy-start | bytes 1572868
  24.1 5.6 %copy-start.9 = (bf16[1024,512]{1,0:T(8,128)(2,1)}, bf16[1024,512]{1,0:T(8,128)(2,1)S(1)}, u32[]{:S(2)}) copy-start(bf16[1024,512]{1,0:T(8,128)(2,1)S(1)} %get-tuple-element.41) | copy-start | bytes 3145732
  24.3 5.4 %copy-start.82 = (f32[256]{0:T(256)}, f32[256]{0:T(256)S(1)}, u32[]{:S(2)}) copy-start(f32[256]{0:T(256)S(1)} %add_rsqrt_fusion.1) | copy-start | bytes 3076
  26.0 3.8 %copy-start.74 = (f32[1024]{0:T(1024)}, f32[1024]{0:T(1024)S(1)}, u32[]{:S(2)}) copy-start(f32[1024]{0:T(1024)S(1)} %pad_maximum_fusion.8) | copy-start | bytes 12292
  32.9 21.9 %copy-start.59 = (bf16[32,2,8,128]{3,2,0,1:T(8,128)(2,1)}, bf16[32,2,8,128]{3,2,0,1:T(8,128)(2,1)S(1)}, u32[]{:S(2)}) copy-start(bf16[32,2,8,128]{3,2,0,1:T(8,128)(2,1)S(1)} %copy.167) | copy-start | bytes 393220
  32.9 20.7 %copy-start.61 = (bf16[32,2,8,128]{3,2,0,1:T(8,128)(2,1)}, bf16[32,2,8,128]{3,2,0,1:T(8,128)(2,1)S(1)}, u32[]{:S(2)}) copy-start(bf16[32,2,8,128]{3,2,0,1:T(8,128)(2,1)S(1)} %copy.166) | copy-start | bytes 393220
  51.7 8.7 %copy-start.2 = (bf16[1024,256]{1,0:T(8,128)(2,1)}, bf16[1024,256]{1,0:T(8,128)(2,1)S(1)}, u32[]{:S(2)}) copy-start(bf16[1024,256]{1,0:T(8,128)(2,1)S(1)} %get-tuple-element.45) | copy-start | bytes 1572868
  54.3 4.0 %copy-start.72 = (f32[512]{0:T(512)}, f32[512]{0:T(512)S(1)}, u32[]{:S(2)}) copy-start(f32[512]{0:T(512)S(1)} %get-tuple-element.175) | copy-start | bytes 6148
  61.9 26.3 %copy-start.68 = (bf16[2,256,128]{1,2,0:T(8,128)(2,1)}, bf16[2,256,128]{1,2,0:T(8,128)(2,1)S(1)}, u32[]{:S(2)}) copy-start(bf16[2,256,128]{1,2,0:T(8,128)(2,1)S(1)} %copy.113) | copy-start | bytes 393220
  88.2 42.6 %copy-start.81 = (f32[256]{0:T(256)}, f32[256]{0:T(256)S(1)}, u32[]{:S(2)}) copy-start(f32[256]{0:T(256)S(1)} %add_rsqrt_fusion) | copy-start | bytes 3076
  130.8 4.6 %copy-start.12 = (bf16[512,1024]{1,0:T(8,128)(2,1)S(1)}, bf16[512,1024]{1,0:T(8,128)(2,1)}, u32[]{:S(2)}) copy-start(bf16[512,1024]{1,0:T(8,128)(2,1)} %copy-done.11) | copy-start | bytes 3145732
  145.6 16.9 %copy-start.58 = (f32[256,128]{0,1:T(8,128)S(1)}, f32[256,128]{0,1:T(8,128)}, u32[]{:S(2)}) copy-start(f32[256,128]{0,1:T(8,128)} %copy.109) | copy-start | bytes 393220
  145.7 16.9 %copy-start.45 = (f32[256,256]{0,1:T(8,128)S(1)}, f32[256,256]{0,1:T(8,128)}, u32[]{:S(2)}) copy-start(f32[256,256]{0,1:T(8,128)} %copy-done.44) | copy-start | bytes 786436
  145.7 16.9 %copy-start.56 = (f32[256,128]{0,1:T(8,128)S(1)}, f32[256,128]{0,1:T(8,128)}, u32[]{:S(2)}) copy-start(f32[256,128]{0,1:T(8,128)} %copy-done.55) | copy-start | bytes 393220
  145.7 16.9 %copy-start.92 = (f32[128]{0:T(128)S(1)}, f32[128]{0:T(128)}, u32[]{:S(2)}) copy-start(f32[128]{0:T(128)} %copy-done.91) | copy-start | bytes 1540
  146.0 17.3 %copy-start.86 = (f32[256,2]{0,1:T(2,128)S(1)}, f32[256,2]{0,1:T(2,128)}, u32[]{:S(2)}) copy-start(f32[256,2]{0,1:T(2,128)} %copy-done.85) | copy-start | bytes 6148
  166.5 6.1 %copy-start.10 = (bf16[1024,512]{1,0:T(8,128)(2,1)S(1)}, bf16[1024,512]{1,0:T(8,128)(2,1)}, u32[]{:S(2)}) copy-start(bf16[1024,512]{1,0:T(8,128)(2,1)} %copy-done.9) | copy-start | bytes 3145732
  168.9 4.4 %copy-start.21 = (bf16[1024,256]{1,0:T(8,128)(2,1)S(1)}, bf16[1024,256]{1,0:T(8,128)(2,1)}, u32[]{:S(2)}) copy-start(bf16[1024,256]{1,0:T(8,128)(2,1)} %copy-done.20) | copy-start | bytes 1572868
  178.0 28.8 %copy-start.93 = (f32[256]{0:T(256)S(1)}, f32[256]{0:T(256)}, u32[]{:S(2)}) copy-start(f32[256]{0:T(256)} %dynamic_slice.30) | copy-start | bytes 3076
  205.0 9.7 %copy-start.23 = (f32[128,768]{1,0:T(8,128)S(1)}, f32[128,768]{1,0:T(8,128)}, u32[]{:S(2)}) copy-start(f32[128,768]{1,0:T(8,128)} %copy-done.22) | copy-start | bytes 1179652
  (72 other events, 124.0 us)
